TPU v7x, 32 devices: a whole 2x2x4 slice. The times are simulated.
32 devices in a mesh: dp: 16 (over z, y, core), tensor: 2 (over x).
Axes of the slice: x: 2, y: 2, z: 4, core: 2. Of those that a mesh axis runs over, the one named last changes fastest.
Arguments:
- tokens: bfloat16 [32768, 1024], P(('dp', 'tensor')), may hold values from -6 to 6
- segment_ids: int32 [16, 2048], P('dp'), may hold values from 0 to 7, never falling along the last dimension, each value on 1 to 800 neighbouring positions
- key_mask: int32 [16, 2048], P('dp'), may hold values 0 or 1
- owners: int32 [48, 1], replicated, may hold values from 0 to 15; in each aligned block of 48 rows (0 to 47, 48 to 95, ...) at most 6 rows name the same one
- master_slots: float32 [2, 96, 128, 1024], P('tensor', 'dp'), may hold values from -0.25 to 0.25
- slot_first: float32 [2, 96, 128, 1024], P('tensor', 'dp'), may hold values from -384 to 384
- slot_second: float32 [2, 96, 128, 1024], P('tensor', 'dp'), may hold values from 2048 to 16384
- vectors: float32 [12, 1024], replicated, may hold values from -0.8 to 1.65, as said below
- vector_first: float32 [12, 1024], replicated, may hold values from -384 to 384
- vector_second: float32 [12, 1024], replicated, may hold values from 2048 to 16384
- out_grad: bfloat16 [32768, 1024], P(('dp', 'tensor')), may hold values from -6 to 6
Outputs:
- layer_out: bfloat16 [32768, 1024], P(('dp', 'tensor'))
- input_grad: bfloat16 [32768, 1024], P(('dp', 'tensor'))
- slot_new: float32 [2, 96, 128, 1024], P('tensor', 'dp')
- slot_first_new: float32 [2, 96, 128, 1024], P('tensor', 'dp')
- slot_second_new: float32 [2, 96, 128, 1024], P('tensor', 'dp')
- vector_new: float32 [12, 1024], replicated
- vector_first_new: float32 [12, 1024], replicated
- vector_second_new: float32 [12, 1024], replicated
Inputs may be any that keep to these rules, and one draw needn't show every extreme that they name: `owners`: no owner holds more than 6 pieces, and some owner holds exactly 6. `segment_ids`: within a sequence the numbers never fall; a document has 1 to 800 tokens, one exactly 800. `vectors`: rows 8 and 10 are positive.
All inputs are finite; a program needn't handle non-finite values. No bound on the sum of `key_mask` on one device may be relied on, other than what follows from the above.
Results may differ from a plain program's by a relative error of at most 0.025.
Values may be sent and summed in bfloat16 or wider, within the bound.
A program may use at most 384 MiB of HBM per device.

v0:
```python
import functools

import jax
import jax.numpy as jnp
from jax import lax
from jax.experimental import pallas as pl
from jax.experimental.pallas import tpu as pltpu
from jax.sharding import PartitionSpec as P

D = 1024
HD = 64
FF = 4096
QBLK = 512
STEP = 10
CAP = 6


norm_eps = 1e-05
mask_fill = -1000000000.0
beta_one = 0.5
beta_two = 0.5
rate_matrix = 0.03
rate_vector = 0.1
weight_decay = 0.01
adam_eps = 1e-08


def slot_index(owners):
    owner_of = owners[:, 0]
    positions = jnp.arange(owner_of.shape[0], dtype=jnp.int32)
    earlier = (positions[None, :] < positions[:, None]) & (owner_of[None, :] == owner_of[:, None])
    within = jnp.sum(earlier.astype(jnp.int32), axis=1)
    return owner_of * CAP + within


def layer_stats(residual):
    center = residual - jnp.mean(residual, axis=-1, keepdims=True)
    spread = jnp.mean(center * center, axis=-1, keepdims=True)
    inverse = lax.rsqrt(spread + norm_eps)
    return (center * inverse, inverse)


def norm_back(grads, normal, inverse, gains):
    scaled = grads * gains
    return inverse * (
        scaled
        - jnp.mean(scaled, axis=-1, keepdims=True)
        - normal * jnp.mean(scaled * normal, axis=-1, keepdims=True)
    )


def gelu_exact(values):
    return jax.nn.gelu(values, approximate=False)


def block_mask(segment, valid, start):
    length = segment.shape[0]
    query_pos = start + jnp.arange(QBLK, dtype=jnp.int32)
    key_pos = jnp.arange(length, dtype=jnp.int32)
    query_seg = lax.dynamic_slice_in_dim(segment, start, QBLK, 0)
    same = query_seg[:, None] == segment[None, :]
    return same & ((valid[None, :] == 1) | (query_pos[:, None] == key_pos[None, :]))


def block_scores(block_q, key_rows, segment, valid, start):
    scores = jnp.einsum("qhd,khd->hqk", block_q, key_rows, preferred_element_type=jnp.float32)
    return jnp.where(block_mask(segment, valid, start)[None], scores, mask_fill)


def attend_forward(queries, key_rows, value_rows, segment, valid):
    length = queries.shape[0]

    def one_block(index):
        start = index * QBLK
        block_q = lax.dynamic_slice_in_dim(queries, start, QBLK, 0)
        scores = block_scores(block_q, key_rows, segment, valid, start)
        row_max = jnp.max(scores, axis=2, keepdims=True)
        raised = jnp.exp(scores - row_max)
        totals = jnp.sum(raised, axis=2, keepdims=True)
        weights = (raised / totals).astype(jnp.bfloat16)
        context = jnp.einsum(
            "hqk,khd->qhd", weights, value_rows, preferred_element_type=jnp.float32
        )
        return (context, (row_max + jnp.log(totals))[:, :, 0])

    context, log_sums = lax.map(one_block, jnp.arange(length // QBLK, dtype=jnp.int32))
    return (context.reshape(length, -1), log_sums)


def attend_backward(queries, key_rows, value_rows, segment, valid, log_sums, grad_context):
    length = queries.shape[0]

    def one_block(carry, index):
        key_acc, value_acc = carry
        start = index * QBLK
        block_q = lax.dynamic_slice_in_dim(queries, start, QBLK, 0)
        block_g = lax.dynamic_slice_in_dim(grad_context, start, QBLK, 0)
        scores = block_scores(block_q, key_rows, segment, valid, start)
        weights = jnp.exp(scores - log_sums[index][:, :, None])
        value_acc = value_acc + jnp.einsum(
            "hqk,qhd->khd",
            weights.astype(jnp.bfloat16),
            block_g,
            preferred_element_type=jnp.float32,
        )
        grad_weights = jnp.einsum(
            "qhd,khd->hqk", block_g, value_rows, preferred_element_type=jnp.float32
        )
        inner = jnp.sum(weights * grad_weights, axis=2, keepdims=True)
        grad_scores = (weights * (grad_weights - inner)).astype(jnp.bfloat16)
        grad_q = jnp.einsum(
            "hqk,khd->qhd", grad_scores, key_rows, preferred_element_type=jnp.float32
        )
        key_acc = key_acc + jnp.einsum(
            "hqk,qhd->khd", grad_scores, block_q, preferred_element_type=jnp.float32
        )
        return ((key_acc, value_acc), grad_q)

    zeros_kv = jnp.zeros(key_rows.shape, jnp.float32)
    (grad_keys, grad_values), grad_queries = lax.scan(
        one_block, (zeros_kv, zeros_kv), jnp.arange(length // QBLK, dtype=jnp.int32)
    )
    return (
        grad_queries.reshape(length, -1),
        grad_keys.reshape(length, -1),
        grad_values.reshape(length, -1),
    )


def adam_update(weights, first, second, grads, rate, decay):
    first_new = beta_one * first + (1.0 - beta_one) * grads
    second_new = beta_two * second + (1.0 - beta_two) * grads * grads
    first_hat = first_new / (1.0 - beta_one**STEP)
    second_hat = second_new / (1.0 - beta_two**STEP)
    updated = weights - rate * (first_hat / (jnp.sqrt(second_hat) + adam_eps) + decay * weights)
    return (updated, first_new, second_new)


def on_device_generic(
    tokens,
    segment_ids,
    key_mask,
    owners,
    master_slots,
    slot_first,
    slot_second,
    vectors,
    vector_first,
    vector_second,
    out_grad,
):
    n_tensor = lax.axis_size("tensor")
    group = lax.axis_index("tensor")
    head_cols = D // n_tensor
    unit_cols = FF // n_tensor
    heads_here = head_cols // HD
    seq_count = segment_ids.shape[0]
    length = segment_ids.shape[1]
    query_scale = HD ** (-0.5)
    slots = slot_index(owners)
    gathered_slots = lax.all_gather(master_slots[0].astype(jnp.bfloat16), "dp", axis=0, tiled=True)
    stack = jnp.take(gathered_slots, slots, axis=0).reshape(-1, D)
    w_mix = stack[0 : 3 * head_cols]
    w_out = stack[3 * head_cols : 4 * head_cols]
    w_up = stack[4 * head_cols : 4 * head_cols + unit_cols]
    w_down = stack[4 * head_cols + unit_cols :]
    bias_query = lax.dynamic_slice_in_dim(vectors[0], group * head_cols, head_cols, 0)
    bias_value = lax.dynamic_slice_in_dim(vectors[1], group * head_cols, head_cols, 0)
    bias_up = lax.dynamic_slice_in_dim(vectors[2:6].reshape(FF), group * unit_cols, unit_cols, 0)
    gathered = lax.all_gather(tokens, "tensor", axis=0, tiled=True)
    mixed = jnp.einsum("ld,kd->lk", gathered, w_mix, preferred_element_type=jnp.float32)
    queries = ((mixed[:, :head_cols] + bias_query) * query_scale).astype(jnp.bfloat16)
    key_rows = mixed[:, head_cols : 2 * head_cols].astype(jnp.bfloat16)
    value_rows = (mixed[:, 2 * head_cols :] + bias_value).astype(jnp.bfloat16)
    head_shape = (seq_count, length, heads_here, HD)
    queries_h = queries.reshape(head_shape)
    keys_h = key_rows.reshape(head_shape)
    values_h = value_rows.reshape(head_shape)

    def forward_seq(element):
        return attend_forward(element[0], element[1], element[2], element[3], element[4])

    context, log_sums = lax.map(forward_seq, (queries_h, keys_h, values_h, segment_ids, key_mask))
    context = context.reshape(-1, head_cols).astype(jnp.bfloat16)
    attn_sum = lax.psum_scatter(
        jnp.einsum("lk,kd->ld", context, w_out, preferred_element_type=jnp.float32).astype(
            jnp.bfloat16
        ),
        "tensor",
        scatter_dimension=0,
        tiled=True,
    ).astype(jnp.float32)
    residual_one = tokens.astype(jnp.float32) + (attn_sum + vectors[6])
    normal_one, inverse_one = layer_stats(residual_one)
    normed = normal_one * vectors[8] + vectors[9]
    normed_low = normed.astype(jnp.bfloat16)
    norm_rows = lax.all_gather(normed_low, "tensor", axis=0, tiled=True)
    hidden_pre = (
        jnp.einsum("ld,kd->lk", norm_rows, w_up, preferred_element_type=jnp.float32) + bias_up
    )
    hidden_full, gelu_pull = jax.vjp(gelu_exact, hidden_pre)
    hidden = hidden_full.astype(jnp.bfloat16)
    mlp_sum = lax.psum_scatter(
        jnp.einsum("lk,kd->ld", hidden, w_down, preferred_element_type=jnp.float32).astype(
            jnp.bfloat16
        ),
        "tensor",
        scatter_dimension=0,
        tiled=True,
    ).astype(jnp.float32)
    residual_two = normed + (mlp_sum + vectors[7])
    normal_two, inverse_two = layer_stats(residual_two)
    layer_out = (normal_two * vectors[10] + vectors[11]).astype(jnp.bfloat16)
    grad_out = out_grad.astype(jnp.float32)
    grad_two = norm_back(grad_out, normal_two, inverse_two, vectors[10])
    grad_down_in = lax.all_gather(grad_two.astype(jnp.bfloat16), "tensor", axis=0, tiled=True)
    grad_hidden = jnp.einsum("ld,kd->lk", grad_down_in, w_down, preferred_element_type=jnp.float32)
    grad_w_down = jnp.einsum("lk,ld->kd", hidden, grad_down_in, preferred_element_type=jnp.float32)
    grad_pre = gelu_pull(grad_hidden)[0].astype(jnp.bfloat16)
    norm_back_rows = lax.all_gather(normed_low, "tensor", axis=0, tiled=True)
    grad_w_up = jnp.einsum(
        "lk,ld->kd", grad_pre, norm_back_rows, preferred_element_type=jnp.float32
    )
    grad_norm = grad_two + lax.psum_scatter(
        jnp.einsum("lk,kd->ld", grad_pre, w_up, preferred_element_type=jnp.float32).astype(
            jnp.bfloat16
        ),
        "tensor",
        scatter_dimension=0,
        tiled=True,
    ).astype(jnp.float32)
    grad_one = norm_back(grad_norm, normal_one, inverse_one, vectors[8])
    grad_attn_in = lax.all_gather(grad_one.astype(jnp.bfloat16), "tensor", axis=0, tiled=True)
    grad_context = jnp.einsum(
        "ld,kd->lk", grad_attn_in, w_out, preferred_element_type=jnp.float32
    ).astype(jnp.bfloat16)
    grad_w_out = jnp.einsum("lk,ld->kd", context, grad_attn_in, preferred_element_type=jnp.float32)

    def backward_seq(element):
        return attend_backward(
            element[0], element[1], element[2], element[3], element[4], element[5], element[6]
        )

    grad_q, grad_k, grad_v = lax.map(
        backward_seq,
        (
            queries_h,
            keys_h,
            values_h,
            segment_ids,
            key_mask,
            log_sums,
            grad_context.reshape(head_shape),
        ),
    )
    grad_queries = grad_q.reshape(-1, head_cols).astype(jnp.bfloat16) * query_scale
    grad_keys = grad_k.reshape(-1, head_cols).astype(jnp.bfloat16)
    grad_values = grad_v.reshape(-1, head_cols).astype(jnp.bfloat16)
    grad_mix = jnp.concatenate([grad_queries, grad_keys, grad_values], axis=1)
    mix_back_rows = lax.all_gather(tokens, "tensor", axis=0, tiled=True)
    grad_w_mix = jnp.einsum(
        "lk,ld->kd", grad_mix, mix_back_rows, preferred_element_type=jnp.float32
    )
    input_grad = (
        grad_one
        + lax.psum_scatter(
            jnp.einsum("lk,kd->ld", grad_mix, w_mix, preferred_element_type=jnp.float32).astype(
                jnp.bfloat16
            ),
            "tensor",
            scatter_dimension=0,
            tiled=True,
        ).astype(jnp.float32)
    ).astype(jnp.bfloat16)
    query_full = lax.dynamic_update_slice_in_dim(
        jnp.zeros((D,), jnp.float32),
        jnp.sum(grad_queries.astype(jnp.float32), axis=0),
        group * head_cols,
        0,
    )
    value_full = lax.dynamic_update_slice_in_dim(
        jnp.zeros((D,), jnp.float32),
        jnp.sum(grad_values.astype(jnp.float32), axis=0),
        group * head_cols,
        0,
    )
    up_full = lax.dynamic_update_slice_in_dim(
        jnp.zeros((FF,), jnp.float32),
        jnp.sum(grad_pre.astype(jnp.float32), axis=0),
        group * unit_cols,
        0,
    )
    tail_rows = jnp.stack(
        [
            jnp.sum(grad_one, axis=0),
            jnp.sum(grad_two, axis=0),
            jnp.sum(grad_norm * normal_one, axis=0),
            jnp.sum(grad_norm, axis=0),
            jnp.sum(grad_out * normal_two, axis=0),
            jnp.sum(grad_out, axis=0),
        ]
    )
    vector_terms = jnp.concatenate(
        [jnp.stack([query_full, value_full]), up_full.reshape(FF // D, D), tail_rows], axis=0
    )
    vector_grads = lax.psum(vector_terms, ("dp", "tensor"))
    grad_stack = jnp.concatenate([grad_w_mix, grad_w_out, grad_w_up, grad_w_down], axis=0)
    grad_pieces = grad_stack.reshape(slots.shape[0], -1, D)
    spread_slots = (
        jnp.zeros((lax.axis_size("dp") * CAP,) + grad_pieces.shape[1:], jnp.float32)
        .at[slots]
        .set(grad_pieces)
    )
    own_grads = lax.psum_scatter(
        spread_slots.astype(jnp.bfloat16), "dp", scatter_dimension=0, tiled=True
    ).astype(jnp.float32)
    slot_new, slot_first_new, slot_second_new = adam_update(
        master_slots[0], slot_first[0], slot_second[0], own_grads, rate_matrix, weight_decay
    )
    vector_new, vector_first_new, vector_second_new = adam_update(
        vectors, vector_first, vector_second, vector_grads, rate_vector, 0.0
    )
    return (
        layer_out,
        input_grad,
        slot_new[None],
        slot_first_new[None],
        slot_second_new[None],
        vector_new,
        vector_first_new,
        vector_second_new,
    )


DOC_MAX = 800
EXT_PAD = 512
ABLK = 256
FINE = 128
HPG = 8
AUG = 16
neg_big = -1000000000.0
NN = (((1,), (0,)), ((), ()))
NT = (((1,), (1,)), ((), ()))
TN = (((0,), (0,)), ((), ()))


def mm(a, b, dims):
    return lax.dot_general(a, b, dims, preferred_element_type=jnp.float32)


def attn_fwd_kernel(lo_ref, hi_ref, q_ref, k_ref, v_ref, qaug_ref, kaug_ref, hid_ref, o_ref, lse_ref, kn_ref, m_ref, acc_ref):
    ext = q_ref.shape[1]
    ones = jnp.concatenate(
        [jnp.ones((1, ABLK), jnp.float32), jnp.zeros((AUG - 1, ABLK), jnp.float32)], axis=0
    ).astype(jnp.bfloat16)
    for h in range(HPG):
        rows = slice(h * HD, (h + 1) * HD)
        kn_ref[h] = jnp.concatenate([k_ref[rows, :], kaug_ref[...]], axis=0).T

    def query_block(qb, _):
        lo = lo_ref[qb]
        hi = hi_ref[qb]
        qs = pl.ds(pl.multiple_of(qb * ABLK, ABLK), ABLK)

        @pl.when(hi > lo)
        def _work():
            hidden = hid_ref[0:1, qs]
            for h in range(HPG):
                rows = slice(h * HD, (h + 1) * HD)
                q32 = q_ref[rows, qs].astype(jnp.float32)
                k32 = k_ref[rows, qs].astype(jnp.float32)
                own = jnp.sum(q32 * k32, axis=0, keepdims=True)
                m_ref[h] = jnp.where(hidden > 0.0, own, -1e30)
                acc_ref[h, 0:HD, :] = v_ref[rows, qs].astype(jnp.float32) * hidden
                acc_ref[h, HD:, :] = jnp.broadcast_to(hidden, (AUG, ABLK))

            blocks = (hi - lo + 1) // 2
            origin = jnp.maximum(hi - 2 * blocks, 0) * FINE

            def key_block(kb, _):
                ks = pl.ds(pl.multiple_of(origin + kb * ABLK, FINE), ABLK)
                heads = [slice(h * HD, (h + 1) * HD) for h in range(HPG)]
                scores = [
                    mm(kn_ref[h, ks, :], jnp.concatenate([q_ref[heads[h], qs], qaug_ref[:, qs]], axis=0), NN)
                    for h in range(HPG)
                ]
                olds = [m_ref[h] for h in range(HPG)]
                news = [
                    jnp.maximum(olds[h], jnp.max(scores[h], axis=0, keepdims=True)) for h in range(HPG)
                ]
                raised = [jnp.exp(scores[h] - news[h]).astype(jnp.bfloat16) for h in range(HPG)]
                for h in range(HPG):
                    m_ref[h] = news[h]
                    va = jnp.concatenate([v_ref[heads[h], ks], ones], axis=0)
                    acc_ref[h] = acc_ref[h] * jnp.exp(olds[h] - news[h]) + mm(va, raised[h], NN)
                return 0

            lax.fori_loop(0, blocks, key_block, 0)
            for h in range(HPG):
                rows = slice(h * HD, (h + 1) * HD)
                total = acc_ref[h, HD : HD + 1, :]
                o_ref[rows, qs] = (acc_ref[h, 0:HD, :] * (1.0 / total)).astype(jnp.bfloat16)
                lse_ref[0, h : h + 1, qs] = m_ref[h] + jnp.log(total)

        @pl.when(hi <= lo)
        def _skip():
            o_ref[:, qs] = jnp.zeros((HPG * HD, ABLK), jnp.bfloat16)
            lse_ref[0, :, qs] = jnp.zeros((8, ABLK), jnp.float32)

        return 0

    lax.fori_loop(0, ext // ABLK, query_block, 0)


def attn_bwd_kernel(
    lo_ref, hi_ref, q_ref, k_ref, v_ref, g_ref, c_ref, lse_ref, qaug_ref, kaug_ref, hid_ref,
    out_ref, kn_ref, vn_ref, acc_ref, dk_acc, dv_acc,
):
    ext = q_ref.shape[1]
    for h in range(HPG):
        rows = slice(h * HD, (h + 1) * HD)
        kn_ref[h] = jnp.concatenate([k_ref[rows, :], kaug_ref[...]], axis=0).T
        vn_ref[h] = v_ref[rows, :].T
    dk_acc[...] = jnp.zeros_like(dk_acc)
    dv_acc[...] = jnp.zeros_like(dv_acc)

    def query_block(qb, _):
        lo = lo_ref[qb]
        hi = hi_ref[qb]
        qs = pl.ds(pl.multiple_of(qb * ABLK, ABLK), ABLK)

        @pl.when(hi > lo)
        def _work():
            hidden = hid_ref[0:1, qs]
            deltas = []
            logs = []
            for h in range(HPG):
                rows = slice(h * HD, (h + 1) * HD)
                q32 = q_ref[rows, qs].astype(jnp.float32)
                k32 = k_ref[rows, qs].astype(jnp.float32)
                v32 = v_ref[rows, qs].astype(jnp.float32)
                g32 = g_ref[rows, qs].astype(jnp.float32)
                c32 = c_ref[rows, qs].astype(jnp.float32)
                delta = jnp.sum(g32 * c32, axis=0, keepdims=True)
                log = lse_ref[0, h : h + 1, qs]
                own = jnp.sum(q32 * k32, axis=0, keepdims=True)
                p_own = jnp.where(hidden > 0.0, jnp.exp(own - log), 0.0)
                d_own = p_own * (jnp.sum(g32 * v32, axis=0, keepdims=True) - delta)
                acc_ref[h] = d_own * k32
                dk_acc[rows, qs] += d_own * q32
                dv_acc[rows, qs] += p_own * g32
                deltas.append(delta)
                logs.append(log)

            blocks = (hi - lo + 1) // 2
            origin = jnp.maximum(hi - 2 * blocks, 0) * FINE

            def key_block(kb, _):
                ks = pl.ds(pl.multiple_of(origin + kb * ABLK, FINE), ABLK)
                heads = [slice(h * HD, (h + 1) * HD) for h in range(HPG)]
                every = range(HPG)
                qs_h = [q_ref[heads[h], qs] for h in every]
                gs_h = [g_ref[heads[h], qs] for h in every]
                scores = [
                    mm(kn_ref[h, ks, :], jnp.concatenate([qs_h[h], qaug_ref[:, qs]], axis=0), NN)
                    for h in every
                ]
                grads = [mm(vn_ref[h, ks, :], gs_h[h], NN) for h in every]
                weights = [jnp.exp(scores[h] - logs[h]) for h in every]
                low = [weights[h].astype(jnp.bfloat16) for h in every]
                back = [
                    (weights[h] * (grads[h] - deltas[h])).astype(jnp.bfloat16) for h in every
                ]
                v_new = [mm(gs_h[h], low[h], NT) for h in every]
                k_new = [mm(qs_h[h], back[h], NT) for h in every]
                q_new = [mm(k_ref[heads[h], ks], back[h], NN) for h in every]
                for h in every:
                    dv_acc[heads[h], ks] += v_new[h]
                    dk_acc[heads[h], ks] += k_new[h]
                    acc_ref[h] += q_new[h]
                return 0

            lax.fori_loop(0, blocks, key_block, 0)
            for h in range(HPG):
                rows = slice(h * HD, (h + 1) * HD)
                out_ref[0, rows, qs] = acc_ref[h].astype(jnp.bfloat16) * (HD ** (-0.5))

        @pl.when(hi <= lo)
        def _skip():
            out_ref[0, :, qs] = jnp.zeros((HPG * HD, ABLK), jnp.bfloat16)

        return 0

    lax.fori_loop(0, ext // ABLK, query_block, 0)
    out_ref[1] = dk_acc[...].astype(jnp.bfloat16)
    out_ref[2] = dv_acc[...].astype(jnp.bfloat16)


def group_block(offset, rows, ext):
    return pl.BlockSpec((rows, ext), lambda g, lo, hi: (offset + g, 0))


def fixed_block(rows, ext):
    return pl.BlockSpec((rows, ext), lambda g, lo, hi: (0, 0))


def attend(lo, hi, qkv, qaug, kaug, hidden):
    ext = qkv.shape[1]
    groups = D // HD // HPG
    rows = HPG * HD
    return pl.pallas_call(
        attn_fwd_kernel,
        out_shape=(
            jax.ShapeDtypeStruct((D, ext), jnp.bfloat16),
            jax.ShapeDtypeStruct((groups, 8, ext), jnp.float32),
        ),
        grid_spec=pltpu.PrefetchScalarGridSpec(
            num_scalar_prefetch=2,
            grid=(groups,),
            in_specs=[
                group_block(0, rows, ext),
                group_block(groups, rows, ext),
                group_block(2 * groups, rows, ext),
                fixed_block(AUG, ext),
                fixed_block(AUG, ext),
                fixed_block(8, ext),
            ],
            out_specs=[
                group_block(0, rows, ext),
                pl.BlockSpec((1, 8, ext), lambda g, lo, hi: (g, 0, 0)),
            ],
            scratch_shapes=[
                pltpu.VMEM((HPG, ext, HD + AUG), jnp.bfloat16),
                pltpu.VMEM((HPG, 1, ABLK), jnp.float32),
                pltpu.VMEM((HPG, HD + AUG, ABLK), jnp.float32),
            ],
        ),
        compiler_params=pltpu.CompilerParams(vmem_limit_bytes=40 * 2**20),
        cost_estimate=pl.CostEstimate(flops=20 * 10**9, bytes_accessed=14 * 10**6, transcendentals=0),
        name="attend",
    )(lo, hi, qkv, qkv, qkv, qaug, kaug, hidden)


def attend_back(lo, hi, qkv, grads, context, logs, qaug, kaug, hidden):
    ext = qkv.shape[1]
    groups = D // HD // HPG
    rows = HPG * HD
    return pl.pallas_call(
        attn_bwd_kernel,
        out_shape=jax.ShapeDtypeStruct((3, D, ext), jnp.bfloat16),
        grid_spec=pltpu.PrefetchScalarGridSpec(
            num_scalar_prefetch=2,
            grid=(groups,),
            in_specs=[
                group_block(0, rows, ext),
                group_block(groups, rows, ext),
                group_block(2 * groups, rows, ext),
                group_block(0, rows, ext),
                group_block(0, rows, ext),
                pl.BlockSpec((1, 8, ext), lambda g, lo, hi: (g, 0, 0)),
                fixed_block(AUG, ext),
                fixed_block(AUG, ext),
                fixed_block(8, ext),
            ],
            out_specs=pl.BlockSpec((3, rows, ext), lambda g, lo, hi: (0, g, 0)),
            scratch_shapes=[
                pltpu.VMEM((HPG, ext, HD + AUG), jnp.bfloat16),
                pltpu.VMEM((HPG, ext, HD), jnp.bfloat16),
                pltpu.VMEM((HPG, HD, ABLK), jnp.float32),
                pltpu.VMEM((rows, ext), jnp.float32),
                pltpu.VMEM((rows, ext), jnp.float32),
            ],
        ),
        compiler_params=pltpu.CompilerParams(vmem_limit_bytes=48 * 2**20),
        cost_estimate=pl.CostEstimate(flops=50 * 10**9, bytes_accessed=30 * 10**6, transcendentals=0),
        name="attend_back",
    )(lo, hi, qkv, qkv, qkv, grads, context, logs, qaug, kaug, hidden)


def document_plan(segment, valid, half, rows):
    length = segment.shape[0]
    ext = rows + EXT_PAD
    base = half * EXT_PAD
    position = jnp.arange(length, dtype=jnp.int32)
    documents = jnp.arange(8, dtype=jnp.int32)[:, None]
    one_hot = segment[None, :] == documents
    counts = jnp.sum(one_hot.astype(jnp.int32), axis=1, keepdims=True)
    starts = jnp.sum((segment[None, :] < documents).astype(jnp.int32), axis=1, keepdims=True)
    start = jnp.sum(jnp.where(one_hot, starts, 0), axis=0)
    end = jnp.sum(jnp.where(one_hot, starts + counts, 0), axis=0)
    crossing = (start < rows) & (end > rows)
    left = jnp.max(jnp.where(crossing, rows - start, 0))
    right = jnp.max(jnp.where(crossing, end - rows, 0))
    in_left = position < rows
    work = jnp.where(crossing, 0, end - start)
    left_work = jnp.sum(jnp.where(in_left, work, 0))
    right_work = jnp.sum(jnp.where(in_left, 0, work))
    both_fit = (left <= DOC_MAX // 2) & (right <= DOC_MAX // 2)
    second = jnp.where(both_fit, right_work <= left_work, left <= right)
    worker = jnp.where(second, half == 1, half == 0)
    own = (position >= half * rows) & (position < (half + 1) * rows)
    handled = jnp.where(crossing, worker, own)
    cut = lambda values: lax.dynamic_slice_in_dim(values, base, ext, 0)
    handled_ext = cut(handled)
    begins = jnp.where(handled_ext, cut(start) - base, ext).reshape(-1, ABLK)
    ends = jnp.where(handled_ext, cut(end) - base, 0).reshape(-1, ABLK)
    lo = jnp.min(begins, axis=1) // FINE
    hi = (jnp.max(ends, axis=1) + (FINE - 1)) // FINE
    blank = jnp.max(ends, axis=1) == 0
    lo = jnp.where(blank, 0, lo)
    hi = jnp.where(blank, 0, hi)
    hot = cut(one_hot.T).T
    masked = cut(valid) == 0
    ones = jnp.ones((1, ext), jnp.bfloat16)
    fill = jnp.zeros((AUG - 9, ext), jnp.bfloat16)
    qaug = jnp.concatenate([hot.astype(jnp.bfloat16), ones, fill], axis=0)
    kaug = jnp.concatenate(
        [
            jnp.where(hot, 0.0, neg_big).astype(jnp.bfloat16),
            jnp.where(masked[None, :], neg_big, 0.0).astype(jnp.bfloat16),
            fill,
        ],
        axis=0,
    )
    hidden = jnp.broadcast_to(masked.astype(jnp.float32)[None, :], (8, ext))
    foreign = lax.dynamic_slice_in_dim(crossing & ~worker, half * rows, rows, 0)
    return lo, hi, qaug, kaug, hidden, handled_ext, foreign


def normal_parts(values):
    bell = jnp.exp(values * values * -0.5)
    return (0.5 + 0.5 * lax.erf(values * 0.7071067811865476), bell * 0.3989422804014327)


UNITS = 1024
STRIP = 512


def up_kernel(x_ref, w_ref, bias_ref, gelu_ref, slope_ref):
    for r in range(0, x_ref.shape[0], STRIP):
        strip = slice(r, r + STRIP)
        values = mm(x_ref[strip, :], w_ref[...], NT) + bias_ref[...]
        cdf, bell = normal_parts(values)
        gelu_ref[strip, :] = (values * cdf).astype(jnp.bfloat16)
        slope_ref[strip, :] = (cdf + values * bell).astype(jnp.bfloat16)


def feed_up(rows, weights, bias):
    length = rows.shape[0]
    units = weights.shape[0]
    out = jax.ShapeDtypeStruct((length, units), jnp.bfloat16)
    columns = pl.BlockSpec((length, UNITS), lambda n: (0, n))
    return pl.pallas_call(
        up_kernel,
        out_shape=(out, out),
        grid=(units // UNITS,),
        in_specs=[
            pl.BlockSpec((length, D), lambda n: (0, 0)),
            pl.BlockSpec((UNITS, D), lambda n: (n, 0)),
            pl.BlockSpec((1, UNITS), lambda n: (0, n)),
        ],
        out_specs=(columns, columns),
        compiler_params=pltpu.CompilerParams(vmem_limit_bytes=40 * 2**20),
        cost_estimate=pl.CostEstimate(
            flops=2 * length * units * D, bytes_accessed=26 * 10**6, transcendentals=0
        ),
        name="feed_up",
    )(rows, weights, bias.reshape(1, units))


def down_back_kernel(g_ref, w_ref, slope_ref, out_ref, sum_ref):
    total = jnp.zeros((1, UNITS), jnp.float32)
    for r in range(0, g_ref.shape[0], STRIP):
        strip = slice(r, r + STRIP)
        grads = mm(g_ref[strip, :], w_ref[...], NT) * slope_ref[strip, :].astype(jnp.float32)
        low = grads.astype(jnp.bfloat16)
        out_ref[strip, :] = low
        total += jnp.sum(low.astype(jnp.float32), axis=0, keepdims=True)
    sum_ref[...] = total


def feed_down_back(grads, weights, slope):
    length = grads.shape[0]
    units = weights.shape[0]
    columns = pl.BlockSpec((length, UNITS), lambda n: (0, n))
    one_row = pl.BlockSpec((1, UNITS), lambda n: (0, n))
    return pl.pallas_call(
        down_back_kernel,
        out_shape=(
            jax.ShapeDtypeStruct((length, units), jnp.bfloat16),
            jax.ShapeDtypeStruct((1, units), jnp.float32),
        ),
        grid=(units // UNITS,),
        in_specs=[
            pl.BlockSpec((length, D), lambda n: (0, 0)),
            pl.BlockSpec((UNITS, D), lambda n: (n, 0)),
            columns,
        ],
        out_specs=(columns, one_row),
        compiler_params=pltpu.CompilerParams(vmem_limit_bytes=40 * 2**20),
        cost_estimate=pl.CostEstimate(
            flops=2 * length * units * D, bytes_accessed=26 * 10**6, transcendentals=0
        ),
        name="feed_down_back",
    )(grads, weights, slope)


MESH = pl.DeviceIdType.MESH
CHUNKS = 3
GROUPS = ((0, 3), (3, 1), (4, 4))
PARTS = (((0, 1), (1, 2)), ((0, 1), None), ((0, 2), (2, 2)))


def neighbours(z, y, core, x):
    def at(z, y, core, x):
        return {"dp": (z * 2 + y) * 2 + core, "tensor": x}

    return {
        "x": at(z, y, core, 1 - x),
        "y": at(z, 1 - y, core, x),
        "core": at(z, y, 1 - core, x),
        "up": at(jnp.minimum(z + 1, 3), y, core, x),
        "down": at(jnp.maximum(z - 1, 0), y, core, x),
    }


def greet(near, z):
    barrier = pltpu.get_barrier_semaphore()
    for name in ("x", "y", "core"):
        pl.semaphore_signal(barrier, inc=1, device_id=near[name], device_id_type=MESH)

    @pl.when(z < 3)
    def _up():
        pl.semaphore_signal(barrier, inc=1, device_id=near["up"], device_id_type=MESH)

    @pl.when(z > 0)
    def _down():
        pl.semaphore_signal(barrier, inc=1, device_id=near["down"], device_id_type=MESH)

    at_end = jnp.where((z == 0) | (z == 3), 1, 0)
    pl.semaphore_wait(barrier, 5 - at_end)


def greet_all(near, me, n_dp):
    barrier = pltpu.get_barrier_semaphore()
    pl.semaphore_signal(barrier, inc=1, device_id=near["x"], device_id_type=MESH)

    def one(i, _):
        other = {"dp": lax.rem(me + i, n_dp), "tensor": lax.axis_index("tensor")}
        pl.semaphore_signal(barrier, inc=1, device_id=other, device_id_type=MESH)
        return 0

    lax.fori_loop(1, n_dp, one, 0)
    pl.semaphore_wait(barrier, n_dp)


def gather_kernel(
    owners_ref, slots_ref, tokens_ref, qkv_ref, out_ref, up_ref, down_ref, ext_ref,
    slot_ref, low_ref, spread_ref, dense_ref, zero_ref, local_sem, own_sem, ext_sem, post, mail, send, recv, halo_send, halo_recv,
):
    z, y, core, x = coordinates()
    near = neighbours(z, y, core, x)
    width = D // 2
    me = lax.axis_index("dp")
    n_dp = low_ref.shape[0]
    for to in range(n_dp):
        lines = slice((to // 2) * 16, (to // 2) * 16 + 16)
        columns = slice((to % 2) * width, (to % 2) * width + width)
        low_ref[to] = slots_ref[:, lines, columns].astype(low_ref.dtype)
    greet_all(near, me, n_dp)

    def letter(to):
        return pltpu.make_async_remote_copy(
            src_ref=low_ref.at[to],
            dst_ref=spread_ref.at[pl.ds(me * CAP, CAP)],
            send_sem=post.at[to],
            recv_sem=mail.at[me],
            device_id={"dp": to, "tensor": x},
            device_id_type=MESH,
        )

    def answer(of):
        return pltpu.make_async_remote_copy(
            src_ref=low_ref.at[of],
            dst_ref=spread_ref.at[pl.ds(of * CAP, CAP)],
            send_sem=post.at[of],
            recv_sem=mail.at[of],
            device_id={"dp": of, "tensor": x},
            device_id_type=MESH,
        )

    def peer(i):
        return lax.rem(me + i, n_dp)

    def post_one(i, _):
        letter(peer(i)).start()
        return 0

    lax.fori_loop(1, n_dp, post_one, 0)

    rows = tokens_ref.shape[0]
    halo = DOC_MAX // 2
    blank = zero_ref.shape[0]
    zero_ref[...] = jnp.zeros_like(zero_ref)
    edge = pl.multiple_of(jnp.where(x == 0, rows - halo, 0), 16)
    there = pl.multiple_of(jnp.where(x == 0, EXT_PAD - halo, rows), 16)
    rest = pl.multiple_of(jnp.where(x == 0, rows + halo, 0), 16)
    border = pltpu.make_async_remote_copy(
        src_ref=tokens_ref.at[pl.ds(edge, halo)],
        dst_ref=ext_ref.at[pl.ds(there, halo)],
        send_sem=halo_send,
        recv_sem=halo_recv,
        device_id=near["x"],
        device_id_type=MESH,
    )
    border.start()
    inside = pltpu.make_async_copy(
        tokens_ref, ext_ref.at[pl.ds(pl.multiple_of(x * EXT_PAD, 16), rows)], ext_sem.at[0]
    )
    inside.start()
    empty = pltpu.make_async_copy(zero_ref, ext_ref.at[pl.ds(rest, blank)], ext_sem.at[1])
    empty.start()
    mine = pltpu.make_async_copy(low_ref.at[me], spread_ref.at[pl.ds(me * CAP, CAP)], local_sem)
    mine.start()
    mine.wait()

    def find(p, _):
        owner = owners_ref[p]

        def count(q, before):
            return before + jnp.where(owners_ref[q] == owner, 1, 0)

        slot_ref[p] = owner * CAP + lax.fori_loop(0, p, count, 0)
        return 0

    lax.fori_loop(0, owners_ref.shape[0], find, 0)

    def mail_one(i, _):
        answer(peer(i)).wait_recv()
        letter(peer(i)).wait_send()
        return 0

    lax.fori_loop(1, n_dp, mail_one, 0)

    def place(p, _):
        dense_ref[p // 4, p % 4] = spread_ref[slot_ref[p]]
        return 0

    lax.fori_loop(0, owners_ref.shape[0], place, 0)
    rest_groups = pl.ds(GROUPS[-1][0] + GROUPS[-1][1], 4)
    later = pltpu.make_async_copy(dense_ref.at[rest_groups], down_ref, local_sem)
    later.start()
    later.wait()

    def block(k, t, zz, yy, cc, part=None):
        groups = slice(None) if part is None else pl.ds(*PARTS[k][part])
        return (qkv_ref, out_ref, up_ref)[k].at[
            groups,
            t,
            :,
            pl.ds(pl.multiple_of((zz * 2 + yy) * 16, 16), 16),
            pl.ds(pl.multiple_of(cc * width, width), width),
        ]

    own = [
        pltpu.make_async_copy(dense_ref.at[pl.ds(*GROUPS[k])], block(k, x, z, y, core), own_sem.at[k])
        for k in range(CHUNKS)
    ]
    for one in own:
        one.start()

    def copy(kind, link, k, zz, t, yy, cc, part=None, fresh=False):
        view = block(k, t, zz, yy, cc, part)
        return pltpu.make_async_remote_copy(
            src_ref=dense_ref.at[pl.ds(*GROUPS[k])] if fresh else view,
            dst_ref=view,
            send_sem=send.at[kind, k, zz],
            recv_sem=recv.at[kind, k, zz],
            device_id=near[link],
            device_id_type=MESH,
        )

    def up(k, zz, fresh=False):
        return copy(0, "up", k, zz, x, y, core, fresh=fresh)

    def down(k, zz, fresh=False):
        return copy(1, "down", k, zz, x, y, core, fresh=fresh)

    def spread(k, zz, fresh):
        copy(2, "x", k, zz, x, y, core, fresh=fresh).start()
        copy(3, "y", k, zz, x, y, core, fresh=fresh).start()
        copy(4, "core", k, zz, x, y, core, fresh=fresh).start()

    def each(d, body):
        @pl.when((d > 0) & (z - d >= 0))
        def _below():
            for k in range(CHUNKS):
                body(k, z - d, 0)

        @pl.when((d > 0) & (z + d <= 3))
        def _above():
            for k in range(CHUNKS):
                body(k, z + d, 1)

    def each_or_own(d, body):
        each(d, body)

        @pl.when(d == 0)
        def _own():
            for k in range(CHUNKS):
                body(k, z, None)

    def begin(k):
        @pl.when(z < 3)
        def _up():
            up(k, z, True).start()

        @pl.when(z > 0)
        def _down():
            down(k, z, True).start()

        spread(k, z, True)

    def first(k, zz, side):
        if side == 0:
            up(k, zz).wait_recv()

            @pl.when(z < 3)
            def _up():
                up(k, zz).start()

        else:
            down(k, zz).wait_recv()

            @pl.when(z > 0)
            def _on():
                down(k, zz).start()

        spread(k, zz, False)

    def second(k, zz, side):
        copy(2, "x", k, zz, 1 - x, y, core).wait_recv()
        copy(5, "y", k, zz, 1 - x, y, core, 0).start()
        copy(7, "core", k, zz, 1 - x, y, core).start()
        copy(3, "y", k, zz, x, 1 - y, core).wait_recv()
        if PARTS[k][1]:
            copy(6, "x", k, zz, x, 1 - y, core, 1).start()
        copy(8, "core", k, zz, x, 1 - y, core).start()

    def third(k, zz, side):
        copy(5, "y", k, zz, 1 - x, 1 - y, core, 0).wait_recv()
        copy(9, "core", k, zz, 1 - x, 1 - y, core, 0).start()
        if PARTS[k][1]:
            copy(6, "x", k, zz, 1 - x, 1 - y, core, 1).wait_recv()
            copy(10, "core", k, zz, 1 - x, 1 - y, core, 1).start()

    def finish(k, zz, side):
        if side != 1:

            @pl.when(z < 3)
            def _up():
                up(k, zz).wait_send()

        if side != 0:

            @pl.when(z > 0)
            def _down():
                down(k, zz).wait_send()

        copy(2, "x", k, zz, x, y, core).wait_send()
        copy(3, "y", k, zz, x, y, core).wait_send()
        copy(5, "y", k, zz, 1 - x, y, core, 0).wait_send()
        if PARTS[k][1]:
            copy(6, "x", k, zz, x, 1 - y, core, 1).wait_send()
        copy(4, "core", k, zz, x, y, core).wait_send()
        copy(7, "core", k, zz, 1 - x, y, core).wait_send()
        copy(8, "core", k, zz, x, 1 - y, core).wait_send()
        copy(9, "core", k, zz, 1 - x, 1 - y, core, 0).wait_send()
        if PARTS[k][1]:
            copy(10, "core", k, zz, 1 - x, 1 - y, core, 1).wait_send()
        copy(4, "core", k, zz, x, y, 1 - core).wait_recv()
        copy(7, "core", k, zz, 1 - x, y, 1 - core).wait_recv()
        copy(8, "core", k, zz, x, 1 - y, 1 - core).wait_recv()
        copy(9, "core", k, zz, 1 - x, 1 - y, 1 - core, 0).wait_recv()
        if PARTS[k][1]:
            copy(10, "core", k, zz, 1 - x, 1 - y, 1 - core, 1).wait_recv()

    for k in range(CHUNKS):
        begin(k)

    def step(d, _):
        @pl.when(d < 4)
        def _one():
            each(d, first)

        @pl.when((d >= 1) & (d < 5))
        def _two():
            each_or_own(d - 1, second)

        @pl.when(d >= 2)
        def _three():
            each_or_own(d - 2, third)

        return 0

    lax.fori_loop(1, 6, step, 0)

    def end(d, _):
        each_or_own(d, finish)
        return 0

    lax.fori_loop(0, 4, end, 0)
    for one in own:
        one.wait()
    border.wait()
    inside.wait()
    empty.wait()


def gather_weights(owners, slots, tokens):
    n_dp = lax.axis_size("dp")
    low = jnp.bfloat16
    rows = tokens.shape[0]
    anywhere = pl.BlockSpec(memory_space=pl.ANY)
    return pl.pallas_call(
        gather_kernel,
        out_shape=tuple(
            jax.ShapeDtypeStruct((count, 2, 4, 128, D), low) for first, count in GROUPS
        )
        + (
            jax.ShapeDtypeStruct((4, 4, 16, D // 2), low),
            jax.ShapeDtypeStruct((rows + EXT_PAD, D), tokens.dtype),
        ),
        in_specs=[
            pl.BlockSpec(memory_space=pltpu.SMEM),
            pl.BlockSpec(memory_space=pltpu.VMEM),
            anywhere,
        ],
        out_specs=(anywhere,) * 5,
        scratch_shapes=[
            pltpu.SMEM(owners.shape, jnp.int32),
            pltpu.VMEM((n_dp, CAP, 16, D // 2), low),
            pltpu.VMEM((n_dp * CAP, 16, D // 2), low),
            pltpu.VMEM((12, 4, 16, D // 2), low),
            pltpu.VMEM((EXT_PAD - DOC_MAX // 2, D), tokens.dtype),
            pltpu.SemaphoreType.DMA,
            pltpu.SemaphoreType.DMA((CHUNKS,)),
            pltpu.SemaphoreType.DMA((2,)),
            pltpu.SemaphoreType.DMA((n_dp,)),
            pltpu.SemaphoreType.DMA((n_dp,)),
            pltpu.SemaphoreType.DMA((11, CHUNKS, 4)),
            pltpu.SemaphoreType.DMA((11, CHUNKS, 4)),
            pltpu.SemaphoreType.DMA,
            pltpu.SemaphoreType.DMA,
        ],
        compiler_params=pltpu.CompilerParams(
            collective_id=1, has_side_effects=True, vmem_limit_bytes=32 * 2**20
        ),
        cost_estimate=pl.CostEstimate(flops=0, bytes_accessed=50 * 10**6, transcendentals=0),
        name="gather_weights",
    )(owners, slots, tokens)


def stack_kernel(parts_ref, out_ref):
    for p in range(4):
        for line in range(8):
            for half in range(2):
                columns = slice(half * (D // 2), (half + 1) * (D // 2))
                out_ref[0, 0, p, line, :, columns] = parts_ref[0, line, half, 0, p]


def stack_chunks(parts):
    return pl.pallas_call(
        stack_kernel,
        out_shape=jax.ShapeDtypeStruct((4, 2, 4, 8, 16, D), parts.dtype),
        grid=(4, 2),
        in_specs=[
            pl.BlockSpec((1, 8, 2, 1, 4, 16, D // 2), lambda m, t: (t, 0, 0, m, 0, 0, 0)),
        ],
        out_specs=pl.BlockSpec((1, 1, 4, 8, 16, D), lambda m, t: (m, t, 0, 0, 0, 0)),
        cost_estimate=pl.CostEstimate(flops=0, bytes_accessed=17 * 10**6, transcendentals=0),
        name="stack_chunks",
    )(parts)


BLOCKS = 12
SLICES = 2
STEPS = BLOCKS * SLICES
LAG = 2


def reduce_kernel(
    piece_ref, vec_ref, qkv_ref, ctx_ref, pre_ref, hid_ref, tok_ref, gext_ref, norm_ref, two_ref,
    out_ref, sum_ref,
    tile, tall, ext_rhs, row_rhs, far_buf, near_buf, core_in, x_in, y_in, x2_in, y2_in, line, line_in,
    done, parcel, vec_in, vec_out,
    tile_sem, rhs_sem, local_sem, post, mail, send, recv, vec_send, vec_recv,
):
    z, y, core, x = coordinates()
    near = neighbours(z, y, core, x)
    me = lax.axis_index("dp")
    n_dp = parcel.shape[1]
    half_width = D // 2
    width = half_width // SLICES
    rows = tile.shape[1]
    tiles = 1024 // rows

    def right(n, half, cut):
        ref = (tok_ref, gext_ref, norm_ref, two_ref)[n]
        to = ext_rhs.at[n, half, cut] if n < 2 else row_rhs.at[n - 2, half, cut]
        which = 1 - core if half == 0 else core
        columns = pl.ds(pl.multiple_of(which * half_width + cut * width, width), width)
        return pltpu.make_async_copy(ref.at[:, columns], to, rhs_sem.at[n, half, cut])

    for cut in range(SLICES):
        for n in range(4):
            for half in range(2):
                right(n, half, cut).start()

    def fetch(n, body):
        i = lax.rem(n // tiles, BLOCKS)
        part = pl.ds(pl.multiple_of(lax.rem(n, tiles) * rows, rows), rows)
        slot = lax.rem(n, 2)
        ext = ext_rhs.shape[3]
        wide = tile.at[slot, :, pl.ds(0, ext)]
        sem = tile_sem.at[slot]

        @pl.when(i < 3)
        def _qkv():
            body(pltpu.make_async_copy(qkv_ref.at[i, part, :], wide, sem))

        @pl.when(i == 3)
        def _out():
            body(pltpu.make_async_copy(ctx_ref.at[part, :], wide, sem))

        def columns(first):
            start = (i - first) * 1024 + lax.rem(n, tiles) * rows
            return pl.ds(pl.multiple_of(start, rows), rows)

        @pl.when((i >= 4) & (i < 8))
        def _up():
            body(pltpu.make_async_copy(pre_ref.at[:, columns(4)], tall.at[slot], sem))

        @pl.when(i >= 8)
        def _down():
            body(pltpu.make_async_copy(hid_ref.at[:, columns(8)], tall.at[slot], sem))

    fetch(0, lambda copy: copy.start())
    greet_all(near, me, n_dp)

    def remote(kind, i, link, src, dst):
        return pltpu.make_async_remote_copy(
            src_ref=src,
            dst_ref=dst,
            send_sem=send.at[kind, i],
            recv_sem=recv.at[kind, i],
            device_id=near[link],
            device_id_type=MESH,
        )

    def core_copy(i):
        return remote(0, i, "core", far_buf.at[lax.rem(i, 2)], core_in.at[i])

    def x1(i):
        return remote(1, i, "x", core_in.at[i, 1 - x, pl.ds(0, 2)], x_in.at[i])

    def y1(i):
        return remote(2, i, "y", core_in.at[i, :, pl.ds(2, 2), :, 1 - y], y_in.at[i])

    def y2(i):
        return remote(3, i, "y", x_in.at[i, :, :, 1 - y], y2_in.at[i])

    def x2(i):
        return remote(4, i, "x", y_in.at[i, 1 - x], x2_in.at[i])

    def along(i, zz):
        return pltpu.make_async_remote_copy(
            src_ref=line.at[i, zz],
            dst_ref=line_in.at[i, z],
            send_sem=send.at[5 + zz, i],
            recv_sem=recv.at[5 + z, i],
            device_id={"dp": (zz * 2 + y) * 2 + core, "tensor": x},
            device_id_type=MESH,
        )

    def arrival(i, zz):
        return pltpu.make_async_remote_copy(
            src_ref=line.at[i, zz],
            dst_ref=line_in.at[i, zz],
            send_sem=send.at[5 + zz, i],
            recv_sem=recv.at[5 + zz, i],
            device_id={"dp": (zz * 2 + y) * 2 + core, "tensor": x},
            device_id_type=MESH,
        )

    def produce(b):
        ring = lax.rem(b, 2)
        cut = b // BLOCKS
        i = lax.rem(b, BLOCKS)

        for c in range(SLICES):
            for n, first in enumerate((0, 3, 4, 8)):

                @pl.when(b == c * BLOCKS + first)
                def _ready():
                    right(n, 0, c).wait()
                    right(n, 1, c).wait()

        @pl.when(b >= 2)
        def _free():
            core_copy(b - 2).wait_send()

        def one(part, _):
            n = b * tiles + part
            slot = lax.rem(n, 2)

            @pl.when(n + 1 < STEPS * tiles)
            def _next():
                fetch(n + 1, lambda copy: copy.start())

            fetch(n, lambda copy: copy.wait())
            t, p = part // 2, lax.rem(part, 2) * 2

            def put(value, to):
                to[ring, t, pl.ds(p, 2)] = value.astype(jnp.bfloat16).reshape(2, 4, 2, 16, width)

            @pl.when(i < 4)
            def _wide():
                which = jnp.where(i < 3, 0, 1)
                put(mm(tile[slot], ext_rhs[which, 0, cut], NN), far_buf)
                put(mm(tile[slot], ext_rhs[which, 1, cut], NN), near_buf)

            @pl.when(i >= 4)
            def _tall():
                which = jnp.where(i < 8, 0, 1)
                put(mm(tall[slot], row_rhs[which, 0, cut], TN), far_buf)
                put(mm(tall[slot], row_rhs[which, 1, cut], TN), near_buf)

            return 0

        lax.fori_loop(0, tiles, one, 0)
        core_copy(b).start()

    def stage_one(i):
        core_copy(i).wait_recv()
        ring = lax.rem(i, 2)

        def add(j, _):
            t, p = j // 4, j % 4
            core_in[i, t, p] = core_in[i, t, p] + near_buf[ring, t, p]
            return 0

        lax.fori_loop(0, 8, add, 0)
        x1(i).start()
        y1(i).start()

    def stage_two(i):
        x1(i).wait_recv()
        y1(i).wait_recv()
        for p in range(2):
            x_in[i, p] = x_in[i, p] + core_in[i, x, p]
        for t in range(2):
            for p in range(2):
                y_in[i, t, p] = y_in[i, t, p] + core_in[i, t, 2 + p, :, y]
        y2(i).start()
        x2(i).start()

    def stage_three(i):
        y2(i).wait_recv()
        x2(i).wait_recv()
        for p in range(2):
            line[i, :, p] = x_in[i, p, :, y] + y2_in[i, p]
            line[i, :, 2 + p] = y_in[i, x, p] + x2_in[i, p]
        for n in range(1, 4):
            along(i, lax.rem(z + n, 4)).start()

    def stage_last(b):
        cut = b // BLOCKS
        total = line[b, z].astype(jnp.float32)
        for n in range(1, 4):
            zz = lax.rem(z + n, 4)
            arrival(b, zz).wait_recv()
            total += line_in[b, zz].astype(jnp.float32)
        done[cut, pl.ds(lax.rem(b, BLOCKS) * 4, 4)] = total.astype(jnp.bfloat16)

    def place(of, cut):
        start = (of % 2) * half_width + cut * width
        return out_ref.at[
            :,
            pl.ds(pl.multiple_of((of // 2) * 16, 16), 16),
            pl.ds(pl.multiple_of(start, width), width),
        ]

    def letter(to, cut):
        return pltpu.make_async_remote_copy(
            src_ref=parcel.at[cut, to],
            dst_ref=place(me, cut),
            send_sem=post.at[cut, to],
            recv_sem=mail.at[cut, me],
            device_id={"dp": to, "tensor": x},
            device_id_type=MESH,
        )

    def answer(of, cut):
        return pltpu.make_async_remote_copy(
            src_ref=parcel.at[cut, of],
            dst_ref=place(of, cut),
            send_sem=post.at[cut, of],
            recv_sem=mail.at[cut, of],
            device_id={"dp": of, "tensor": x},
            device_id_type=MESH,
        )

    def own_letter(cut):
        return pltpu.make_async_copy(parcel.at[cut, me], place(me, cut), local_sem.at[cut])

    def post_all(cut):
        done[cut, BLOCKS * 4] = jnp.zeros((16, width), done.dtype)

        def pack(n, _):
            parcel[cut, n // CAP, n % CAP] = done[cut, piece_ref[n]]
            return 0

        lax.fori_loop(0, n_dp * CAP, pack, 0)

        def post_one(i, _):
            letter(lax.rem(me + i, n_dp), cut).start()
            return 0

        lax.fori_loop(1, n_dp, post_one, 0)
        own_letter(cut).start()

    def ended(i):
        @pl.when(i >= STEPS - 2)
        def _far():
            core_copy(i).wait_send()

        x1(i).wait_send()
        y1(i).wait_send()
        y2(i).wait_send()
        x2(i).wait_send()
        for n in range(1, 4):
            along(i, lax.rem(z + n, 4)).wait_send()

    z_one = z + 1 - 2 * lax.rem(z, 2)
    z_two = lax.rem(z + 2, 4)
    partners = [
        near["core"],
        near["y"],
        near["x"],
        {"dp": (z_one * 2 + y) * 2 + core, "tensor": x},
        {"dp": (z_two * 2 + y) * 2 + core, "tensor": x},
    ]

    def swap(n):
        return pltpu.make_async_remote_copy(
            src_ref=vec_out.at[n],
            dst_ref=vec_in.at[n],
            send_sem=vec_send.at[n],
            recv_sem=vec_recv.at[n],
            device_id=partners[n],
            device_id_type=MESH,
        )

    vec_out[0] = vec_ref[...]
    produce(0)

    def step(s, _):
        @pl.when(s + 1 < STEPS)
        def _produce():
            produce(s + 1)

        @pl.when(s < STEPS)
        def _one():
            stage_one(s)

        @pl.when((s >= LAG) & (s < STEPS + LAG))
        def _two():
            stage_two(s - LAG)

        @pl.when((s >= 2 * LAG) & (s < STEPS + 2 * LAG))
        def _three():
            stage_three(s - 2 * LAG)

        @pl.when(s >= 3 * LAG)
        def _last():
            stage_last(s - 3 * LAG)

        for cut in range(SLICES):

            @pl.when(s - 3 * LAG == cut * BLOCKS + BLOCKS - 1)
            def _post():
                post_all(cut)

        for n in range(5):

            @pl.when(s == n)
            def _begin():
                swap(n).start()

            @pl.when(s == n + 1)
            def _end():
                swap(n).wait()
                if n < 4:
                    vec_out[n + 1] = vec_out[n] + vec_in[n]
                else:
                    sum_ref[...] = vec_out[n] + vec_in[n]

        return 0

    lax.fori_loop(0, STEPS + 3 * LAG, step, 0)

    def finish(i, _):
        ended(i)
        return 0

    lax.fori_loop(0, STEPS, finish, 0)

    def mail_one(i, _):
        for cut in range(SLICES):
            answer(lax.rem(me + i, n_dp), cut).wait_recv()
            letter(lax.rem(me + i, n_dp), cut).wait_send()
        return 0

    lax.fori_loop(1, n_dp, mail_one, 0)
    for cut in range(SLICES):
        own_letter(cut).wait()


def reduce_grads(piece_of, vec, qkv, context, pre, hidden, tokens, ext_grads, normed, two):
    n_dp = piece_of.shape[0] // CAP
    low = jnp.bfloat16
    width = D // 2 // SLICES
    rows = 256
    ext = tokens.shape[0]
    length = normed.shape[0]
    anywhere = pl.BlockSpec(memory_space=pl.ANY)
    vmem = pl.BlockSpec(memory_space=pltpu.VMEM)
    return pl.pallas_call(
        reduce_kernel,
        out_shape=(
            jax.ShapeDtypeStruct((CAP, 128, D), low),
            jax.ShapeDtypeStruct(vec.shape, jnp.float32),
        ),
        in_specs=[pl.BlockSpec(memory_space=pltpu.SMEM), vmem] + [anywhere] * 8,
        out_specs=(anywhere, vmem),
        scratch_shapes=[
            pltpu.VMEM((2, rows, ext), low),
            pltpu.VMEM((2, length, rows), low),
            pltpu.VMEM((2, 2, SLICES, ext, width), low),
            pltpu.VMEM((2, 2, SLICES, length, width), low),
            pltpu.VMEM((2, 2, 4, 4, 2, 16, width), low),
            pltpu.VMEM((2, 2, 4, 4, 2, 16, width), low),
            pltpu.VMEM((STEPS, 2, 4, 4, 2, 16, width), low),
            pltpu.VMEM((STEPS, 2, 4, 2, 16, width), low),
            pltpu.VMEM((STEPS, 2, 2, 4, 16, width), low),
            pltpu.VMEM((STEPS, 2, 4, 16, width), low),
            pltpu.VMEM((STEPS, 2, 4, 16, width), low),
            pltpu.VMEM((STEPS, 4, 4, 16, width), low),
            pltpu.VMEM((STEPS, 4, 4, 16, width), low),
            pltpu.VMEM((SLICES, BLOCKS * 4 + 1, 16, width), low),
            pltpu.VMEM((SLICES, n_dp, CAP, 16, width), low),
            pltpu.VMEM((5,) + vec.shape, jnp.float32),
            pltpu.VMEM((5,) + vec.shape, jnp.float32),
            pltpu.SemaphoreType.DMA((2,)),
            pltpu.SemaphoreType.DMA((4, 2, SLICES)),
            pltpu.SemaphoreType.DMA((SLICES,)),
            pltpu.SemaphoreType.DMA((SLICES, n_dp)),
            pltpu.SemaphoreType.DMA((SLICES, n_dp)),
            pltpu.SemaphoreType.DMA((9, STEPS)),
            pltpu.SemaphoreType.DMA((9, STEPS)),
            pltpu.SemaphoreType.DMA((5,)),
            pltpu.SemaphoreType.DMA((5,)),
        ],
        compiler_params=pltpu.CompilerParams(
            collective_id=2, has_side_effects=True, vmem_limit_bytes=60 * 2**20
        ),
        cost_estimate=pl.CostEstimate(
            flops=31 * 10**9, bytes_accessed=50 * 10**6, transcendentals=0
        ),
        name="reduce_grads",
    )(piece_of, vec, qkv, context, pre, hidden, tokens, ext_grads, normed, two)


def coordinates():
    dp = lax.axis_index("dp")
    return dp // 4, (dp // 2) % 2, dp % 2, lax.axis_index("tensor")


def exchange(values, axis):
    if axis == "x":
        return lax.ppermute(values, "tensor", [(0, 1), (1, 0)])
    flip = {"core": 1, "y": 2, "z_near": 4, "z_far": 8}[axis]
    return lax.ppermute(values, "dp", [(i, i ^ flip) for i in range(lax.axis_size("dp"))])


def pick(values, index, axis):
    return lax.dynamic_index_in_dim(values, index, axis, keepdims=False)


def on_device_rows(
    tokens,
    segment_ids,
    key_mask,
    owners,
    master_slots,
    slot_first,
    slot_second,
    vectors,
    vector_first,
    vector_second,
    out_grad,
):
    n_dp = lax.axis_size("dp")
    n_tensor = lax.axis_size("tensor")
    half = lax.axis_index("tensor")
    every = ("tensor", "dp")
    rows = tokens.shape[0]
    ext = rows + EXT_PAD
    halo = DOC_MAX // 2
    swap = [(0, 1), (1, 0)]
    edge = jnp.where(half == 0, rows - halo, 0)
    halo_at = jnp.where(half == 0, rows, EXT_PAD - halo)
    own_at = half * EXT_PAD

    def extend(own_rows, halo_rows):
        whole = jnp.zeros((ext,) + own_rows.shape[1:], own_rows.dtype)
        whole = lax.dynamic_update_slice_in_dim(whole, halo_rows, halo_at, 0)
        return lax.dynamic_update_slice_in_dim(whole, own_rows, own_at, 0)

    def own_part(values):
        return lax.dynamic_slice_in_dim(values, own_at, rows, 0)

    def halo_part(values):
        return lax.dynamic_slice_in_dim(values, halo_at, halo, 0)

    lo, hi, qaug, kaug, hidden_keys, handled, foreign = document_plan(
        segment_ids[0], key_mask[0], half, rows
    )
    slots = slot_index(owners)
    pieces = slots.shape[0]
    piece_rows = master_slots.shape[2]
    mix_pieces = 4 * (D // n_tensor) // piece_rows
    up_pieces = (FF // n_tensor) // piece_rows
    per = mix_pieces // 4
    w_qkv, w_out, w_up, down_chunk, tokens_ext = gather_weights(owners[:, 0], master_slots[0], tokens)
    w_qkv = w_qkv.reshape(3 * D, D)
    w_out = w_out.reshape(D, D)
    w_up = w_up.reshape(FF, D)
    down_chunks = lax.all_gather(down_chunk, every, axis=0, tiled=False)
    w_down = stack_chunks(down_chunks.reshape((n_tensor, 8, 2) + down_chunk.shape)).reshape(FF, D)
    bias_up = vectors[2:6].reshape(n_tensor, 4, -1).transpose(1, 0, 2).reshape(FF)

    bias_qkv = jnp.concatenate([vectors[0], jnp.zeros((D,), jnp.float32), vectors[1]])
    scale_qkv = jnp.concatenate([jnp.full((D,), HD ** (-0.5)), jnp.ones((2 * D,))])
    qkv = (
        (mm(w_qkv, tokens_ext, NT) + bias_qkv[:, None]) * scale_qkv.astype(jnp.float32)[:, None]
    ).astype(jnp.bfloat16)
    context, logs = attend(lo, hi, qkv, qaug, kaug, hidden_keys)
    attn_ext = mm(context, w_out, TN).astype(jnp.bfloat16)
    halo_attn = lax.ppermute(halo_part(attn_ext), "tensor", swap)
    attn_back = lax.dynamic_update_slice_in_dim(
        jnp.zeros((rows, D), jnp.bfloat16), halo_attn, edge, 0
    )
    attn_sum = jnp.where(foreign[:, None], attn_back, own_part(attn_ext)).astype(jnp.float32)
    residual_one = tokens.astype(jnp.float32) + (attn_sum + vectors[6])
    normal_one, inverse_one = layer_stats(residual_one)
    normed = normal_one * vectors[8] + vectors[9]
    normed_low = normed.astype(jnp.bfloat16)

    hidden, slope = feed_up(normed_low, w_up, bias_up)
    residual_two = normed + (mm(hidden, w_down, NN) + vectors[7])
    normal_two, inverse_two = layer_stats(residual_two)
    layer_out = (normal_two * vectors[10] + vectors[11]).astype(jnp.bfloat16)
    grad_out = out_grad.astype(jnp.float32)
    grad_two = norm_back(grad_out, normal_two, inverse_two, vectors[10])
    grad_two_low = grad_two.astype(jnp.bfloat16)

    grad_pre, up_sums = feed_down_back(grad_two_low, w_down, slope)
    grad_norm = grad_two + lax.optimization_barrier(mm(grad_pre, w_up, NN))
    grad_one = norm_back(grad_norm, normal_one, inverse_one, vectors[8])
    grad_one_low = grad_one.astype(jnp.bfloat16)

    halo_grad = lax.ppermute(
        lax.dynamic_slice_in_dim(grad_one_low, edge, halo, 0), "tensor", swap
    )
    grad_ext = jnp.where(handled[:, None], extend(grad_one_low, halo_grad), 0)
    grad_context = mm(w_out, grad_ext, NT).astype(jnp.bfloat16)
    grad_qkv = attend_back(lo, hi, qkv, grad_context, context, logs, qaug, kaug, hidden_keys)
    input_ext = mm(grad_qkv.reshape(3 * D, ext), w_qkv, TN)
    halo_input = lax.ppermute(halo_part(input_ext).astype(jnp.bfloat16), "tensor", swap)
    input_back = lax.dynamic_update_slice_in_dim(
        jnp.zeros((rows, D), jnp.bfloat16), halo_input, edge, 0
    )
    input_grad = (grad_one + own_part(input_ext) + input_back.astype(jnp.float32)).astype(
        jnp.bfloat16
    )

    vector_terms = jnp.concatenate(
        [
            jnp.stack(
                [
                    jnp.sum(grad_qkv[0].astype(jnp.float32), axis=1),
                    jnp.sum(grad_qkv[2].astype(jnp.float32), axis=1),
                ]
            ),
            up_sums.reshape(4, n_tensor, -1)
            .transpose(1, 0, 2)
            .reshape(FF // D, D),
            jnp.stack(
                [
                    jnp.sum(grad_one, axis=0),
                    jnp.sum(grad_two, axis=0),
                    jnp.sum(grad_norm * normal_one, axis=0),
                    jnp.sum(grad_norm, axis=0),
                    jnp.sum(grad_out * normal_two, axis=0),
                    jnp.sum(grad_out, axis=0),
                ]
            ),
        ],
        axis=0,
    )
    piece_of = jnp.full((n_dp * CAP,), pieces, jnp.int32).at[slots].set(
        jnp.arange(pieces, dtype=jnp.int32)
    )
    own_grads, vector_grads = reduce_grads(
        piece_of,
        vector_terms,
        grad_qkv,
        context,
        grad_pre,
        hidden,
        tokens_ext,
        grad_ext,
        normed_low,
        grad_two_low,
    )
    own_grads = own_grads.astype(jnp.float32)
    slot_new, slot_first_new, slot_second_new = adam_update(
        master_slots[0], slot_first[0], slot_second[0], own_grads, rate_matrix, weight_decay
    )
    vector_new, vector_first_new, vector_second_new = adam_update(
        vectors, vector_first, vector_second, vector_grads, rate_vector, 0.0
    )
    return (
        layer_out,
        input_grad,
        slot_new[None],
        slot_first_new[None],
        slot_second_new[None],
        vector_new,
        vector_first_new,
        vector_second_new,
    )


def solution(mesh):
    placed = (
        P(("dp", "tensor"), None),
        P("dp", None),
        P("dp", None),
        P(),
        P("tensor", "dp", None, None),
        P("tensor", "dp", None, None),
        P("tensor", "dp", None, None),
        P(),
        P(),
        P(),
        P(("dp", "tensor"), None),
    )
    by_rows = mesh.shape["tensor"] == 2 and mesh.shape["dp"] == 16
    return jax.shard_map(
        on_device_rows if by_rows else on_device_generic,
        mesh=mesh,
        in_specs=placed,
        out_specs=(
            P(("dp", "tensor"), None),
            P(("dp", "tensor"), None),
            P("tensor", "dp", None, None),
            P("tensor", "dp", None, None),
            P("tensor", "dp", None, None),
            P(),
            P(),
            P(),
        ),
        check_vma=False,
    )
```

profile of v0, /device:TPU:13, one launch (start us, length us, event | category | flops | bytes accessed | tf_op | source)
XLA Modules:
  0.0 625.7 jit_solution(4104097347205941061)
XLA Ops:
  7.2 1.6 copy-done
  8.8 1.9 copy-done.2
  10.7 0.7 copy-done.6
  11.4 113.7 %gather_weights.1 = (bf16[3,2,4,128,1024]{4,3,2,1,0:T(8,128)(2,1)S(1)}, bf16[1,2,4,128,1024]{4,3,2,1,0:T(8,128)(2,1)S(1)}, bf16[4,2,4,128,1024]{4,3,2,1,0:T(8,12...) custom-call(s32[48]{0:T(128)S(1)} %bitcast.70, f32[6,128,1024]{2,1,0:T(8,128)S(1)} %bitcast.69, ...), custom_call_target="tpu_custom_call" | custom-call | bytes 50000000 | tf_op jit(solution)/shard_map/gather_weights/pallas_call | solution.py:1025
  125.1 2.7 copy-done.8
  127.8 1.3 copy-done.10
  129.5 1.0 select_reduce_fusion.2
  135.3 15.5 %multiply_convert_fusion.q_ref.k_ref.v_ref = bf16[3072,1536]{1,0:T(8,128)(2,1)} fusion(bf16[3072,1024]{1,0:T(8,128)(2,1)} %bitcast.72, bf16[1536,1024]{1,0:T(8,128)(2,1)S(1)} %get-tuple-element.22.tok_ref, f32[3072]{0:T(1024)S(1)} %copy-done.32, f32[3072]{0:T(1024)S(1)} %pad_maximum_fusion), kind=kOutput, calls=%fused_computation.1 | convolution fusion | flops 9677832192 | bytes 18898944 | tf_op jit(solution)/shard_map/dot_general | solution.py:348
  150.8 3.7 copy-done.16
  154.4 36.1 %attend.1 = (bf16[1024,1536]{1,0:T(8,128)(2,1)S(1)}, f32[2,8,1536]{2,1,0:T(8,128)S(1)}) custom-call(s32[6]{0:T(128)S(1)} %get-tuple-element.82.lo_ref, s32[6]{0:T(128)S(1)} %get-tuple-element.81.hi_ref, bf16[3072,1536]{1,0:T(8,128)(2,1)S(1)} %copy-done.16, bf16[3072,1536]{1,0:T(8,128)(2,1)S(1)} %copy-done.16, bf16[3072,1536]{1,0:T(8,128)(2,1)S(1)} %copy-done.16, ...), custom_call_target="tpu_custom_call" | custom-call | flops 20000000000 | bytes 14000000 | tf_op jit(solution)/shard_map/attend/pallas_call | solution.py:511
  190.6 3.7 convolution_convert_fusion.1
  194.4 1.0 constant_dynamic-slice_fusion.1
  195.3 1.1 copy-done.25
  196.5 12.2 %collective-permute-done = bf16[400,1024]{1,0:T(8,128)(2,1)S(1)} collective-permute-done((bf16[400,1024]{1,0:T(8,128)(2,1)}, bf16[400,1024]{1,0:T(8,128)(2,1)S(1)}, u32[]{:S(2)}, u32[]{:S(2)}) %collective-permute-start) | collective-permute-done | bytes 819232 | tf_op jit(solution)/shard_map/ppermute | solution.py:1561
  209.0 2.3 fusion.8
  211.3 1.0 multiply_reduce_fusion.3
  212.4 1.5 fusion.7.x_ref.norm_ref
  213.9 18.7 %feed_up.1 = (bf16[1024,4096]{1,0:T(8,128)(2,1)S(1)}, bf16[1024,4096]{1,0:T(8,128)(2,1)}) custom-call(bf16[1024,1024]{1,0:T(8,128)(2,1)S(1)} %fusion.7.x_ref.norm_ref, bf16[4096,1024]{1,0:T(8,128)(2,1)} %bitcast.115, f32[1,4096]{1,0:T(1,128)S(1)} %reshape_reshape.3.bias_ref), custom_call_target="tpu_custom_call" | custom-call | flops 8589934592 | bytes 26000000 | tf_op jit(solution)/shard_map/feed_up/pallas_call | solution.py:653
  232.6 1.3 copy-done.5
  233.9 3.2 copy-done.14
  237.2 9.0 %stack_chunks.1 = bf16[4,2,4,8,16,1024]{5,4,3,2,1,0:T(8,128)(2,1)} custom-call(bf16[2,8,2,4,4,16,512]{6,5,4,3,2,1,0:T(8,128)(2,1)} %bitcast.78), custom_call_target="tpu_custom_call" | custom-call | bytes 17000000 | tf_op jit(solution)/shard_map/stack_chunks/pallas_call | solution.py:1073
  246.2 15.0 %fusion.29 = (f32[1024]{0:T(1024)S(1)}, f32[1024,1024]{1,0:T(8,128)S(1)}) fusion(f32[1024]{0:T(1024)S(1)} %bitcast.114, bf16[1024,4096]{1,0:T(8,128)(2,1)} %copy-done.14, bf16[4096,1024]{1,0:T(8,128)(2,1)} %bitcast.79, f32[1024]{0:T(1024)S(1)} %bitcast.111, f32[1024]{0:T(1024)S(1)} %bitcast.96, f32[1024]{0:T(1024)S(1)} %add_rsqrt_fusion.1, ...), kind=kOutput, calls=%fused_computation.111 | convolution fusion | flops 8601467904 | bytes 25194496 | tf_op jit(solution)/shard_map/dot_general | solution.py:348
  261.2 0.6 multiply_reduce_fusion.2
  261.8 1.0 copy-done.22
  262.8 2.2 fusion.6
  265.1 3.2 fusion.24
  268.6 13.7 %feed_down_back.1 = (bf16[1024,4096]{1,0:T(8,128)(2,1)S(1)}, f32[1,4096]{1,0:T(1,128)S(1)}) custom-call(bf16[1024,1024]{1,0:T(8,128)(2,1)S(1)} %convert_element_type.86.g_ref.two_ref, bf16[4096,1024]{1,0:T(8,128)(2,1)} %bitcast.80, bf16[1024,4096]{1,0:T(8,128)(2,1)} %get-tuple-element.28.slope_ref), custom_call_target="tpu_custom_call" | custom-call | flops 8589934592 | bytes 26000000 | tf_op jit(solution)/shard_map/feed_down_back/pallas_call | solution.py:687
  282.3 14.2 %fusion.30 = f32[1024,1024]{1,0:T(8,128)S(1)} fusion(bf16[1024,4096]{1,0:T(8,128)(2,1)S(1)} %get-tuple-element.29.pre_ref, bf16[4096,1024]{1,0:T(8,128)(2,1)} %bitcast.116), kind=kOutput, calls=%fused_computation.112 | convolution fusion | flops 8589934592 | bytes 20971520 | tf_op jit(solution)/shard_map/dot_general | solution.py:348
  296.6 3.5 multiply_reduce_fusion
  300.1 2.0 fusion.26
  303.0 1.2 copy-done.17
  304.2 1.2 scatter_custom_fusion.piece_ref
  305.5 0.5 broadcast.182
  306.0 0.7 reduce.7
  306.7 7.1 %collective-permute-done.1 = bf16[400,1024]{1,0:T(8,128)(2,1)S(1)} collective-permute-done((bf16[400,1024]{1,0:T(8,128)(2,1)S(1)}, bf16[400,1024]{1,0:T(8,128)(2,1)S(1)}, u32[]{:S(2)}, u32[]{:S(2)}) %collective-permute-start.1) | collective-permute-done | bytes 819232 | tf_op jit(solution)/shard_map/ppermute | solution.py:1584
  314.8 1.1 broadcast_select_fusion.gext_ref
  315.9 0.5 copy-done.12
  316.4 3.7 convolution_convert_fusion.g_ref
  320.1 71.2 %attend_back.1.qkv_ref = bf16[3,1024,1536]{2,1,0:T(8,128)(2,1)} custom-call(s32[6]{0:T(128)S(1)} %get-tuple-element.82.lo_ref, s32[6]{0:T(128)S(1)} %get-tuple-element.81.hi_ref, bf16[3072,1536]{1,0:T(8,128)(2,1)} %multiply_convert_fusion.q_ref.k_ref.v_ref, bf16[3072,1536]{1,0:T(8,128)(2,1)} %multiply_convert_fusion.q_ref.k_ref.v_ref, ...), custom_call_target="tpu_custom_call" | custom-call | flops 49999998976 | bytes 30000000 | tf_op jit(solution)/shard_map/attend_back/pallas_call | solution.py:548
  391.2 3.7 convert_reduce_fusion
  395.0 12.8 %fusion.31 = f32[1536,1024]{1,0:T(8,128)S(1)} fusion(bf16[3072,1536]{1,0:T(8,128)(2,1)} %bitcast.81, bf16[3072,1024]{1,0:T(8,128)(2,1)S(1)} %bitcast.75), kind=kOutput, calls=%fused_computation.113 | convolution fusion | flops 9663676416 | bytes 22020096 | tf_op jit(solution)/shard_map/dot_general | solution.py:348
  407.8 2.7 copy-done.23
  410.5 1.0 dynamic-slice_convert_fusion
  411.5 1.3 concatenate.15.vec_ref
  412.8 191.3 %reduce_grads.1 = (bf16[6,128,1024]{2,1,0:T(8,128)(2,1)}, f32[12,1024]{1,0:T(8,128)}) custom-call(s32[96]{0:T(128)} %scatter_custom_fusion.piece_ref, f32[12,1024]{1,0:T(8,128)} %concatenate.15.vec_ref, bf16[3,1024,1536]{2,1,0:T(8,128)(2,1)} %attend_back.1.qkv_ref, bf16[1024,1536]{1,0:T(8,128)(2,1)} %copy-done.15, bf16[1024,4096]{1,0:T(8,128)(2,1)} %copy-done.13, ...), custom_call_target="tpu_custom_call" | custom-call | flops 31000000512 | bytes 50000000 | tf_op jit(solution)/shard_map/reduce_grads/pallas_call | solution.py:1439
  604.1 1.6 multiply_subtract_fusion
  605.7 9.6 %fusion.11 = (f32[1,6,128,1024]{3,2,1,0:T(8,128)}, f32[1,6,128,1024]{3,2,1,0:T(8,128)}, f32[1,6,128,1024]{3,2,1,0:T(8,128)}) fusion(bf16[6,128,1024]{2,1,0:T(8,128)(2,1)} %get-tuple-element.32, f32[1,6,128,1024]{3,2,1,0:T(8,128)} %param.17, f32[1,6,128,1024]{3,2,1,0:T(8,128)} %param.16, f32[1,6,128,1024]{3,2,1,0:T(8,128)S(1)} %copy-done.3), kind=kLoop, calls=%fused_computation.39 | loop fusion | flops 11796480 | bytes 20447232 | tf_op jit(solution)/shard_map/broadcast_in_dim | solution.py:1650
  615.7 2.7 add_convert_fusion
  (120 shorter events, 4.1 us)
Async XLA Ops:
  7.2 230.0 %all-gather.3.cloned.1.call-start = ((), (), s32[]{:S(2)}) async-start(), calls=%async_computation | async-start | bytes 8650752 | tf_op jit(solution)/shard_map/all_gather | solution.py:1550
  7.2 1.6 copy-start
  8.8 1.9 copy-start.2
  10.7 0.7 copy-start.6
  11.4 117.8 %copy-start.29 = (s32[1,2048]{1,0:T(1,128)S(1)}, s32[1,2048]{1,0:T(1,128)}, u32[]{:S(2)}) copy-start(s32[1,2048]{1,0:T(1,128)} %param.12) | copy-start | bytes 24580
  11.4 123.6 %copy-start.31 = (s32[1,2048]{1,0:T(1,128)S(1)}, s32[1,2048]{1,0:T(1,128)}, u32[]{:S(2)}) copy-start(s32[1,2048]{1,0:T(1,128)} %param.13) | copy-start | bytes 24580
  11.4 123.7 %copy-start.27 = (f32[12,1024]{1,0:T(8,128)S(1)}, f32[12,1024]{1,0:T(8,128)}, u32[]{:S(2)}) copy-start(f32[12,1024]{1,0:T(8,128)} %param.18) | copy-start | bytes 147460
  11.4 123.9 %copy-start.32 = (f32[3072]{0:T(1024)S(1)}, f32[3072]{0:T(1024)}, u32[]{:S(2)}) copy-start(f32[3072]{0:T(1024)} %constant.94.clone.1) | copy-start | bytes 36868
  125.1 2.7 copy-start.8
  127.8 1.3 copy-start.10
  129.2 21.6 %copy-start.9 = (bf16[1536,1024]{1,0:T(8,128)(2,1)}, bf16[1536,1024]{1,0:T(8,128)(2,1)S(1)}, u32[]{:S(2)}) copy-start(bf16[1536,1024]{1,0:T(8,128)(2,1)S(1)} %get-tuple-element.22.tok_ref) | copy-start | bytes 9437188
  150.7 3.7 copy-start.16
  154.4 36.1 %copy-start.11 = (bf16[1,2,4,128,1024]{4,3,2,1,0:T(8,128)(2,1)S(1)}, bf16[1,2,4,128,1024]{4,3,2,1,0:T(8,128)(2,1)}, u32[]{:S(2)}) copy-start(bf16[1,2,4,128,1024]{4,3,2,1,0:T(8,128)(2,1)} %copy-done.10) | copy-start | bytes 6291460
  190.6 3.8 copy-start.15
  194.3 2.1 copy-start.25
  194.3 14.7 %copy-start.1 = (bf16[1024,1024]{1,0:T(8,128)(2,1)S(1)}, bf16[1024,1024]{1,0:T(8,128)(2,1)}, u32[]{:S(2)}) copy-start(bf16[1024,1024]{1,0:T(8,128)(2,1)} %tokens_ref.1) | copy-start | bytes 6291460
  196.4 12.3 %collective-permute-start = (bf16[400,1024]{1,0:T(8,128)(2,1)}, bf16[400,1024]{1,0:T(8,128)(2,1)S(1)}, u32[]{:S(2)}, u32[]{:S(2)}) collective-permute-start(bf16[400,1024]{1,0:T(8,128)(2,1)} %constant_dynamic-slice_fusion.1), channel_id=1, source_target_pairs={{0,1},{1,0},{2,3},{3,2},{4,5},{5,4},{6,7},{7,6},{8,9},{9,8},{10,11... | collective-permute-start | bytes 2457608 | tf_op jit(solution)/shard_map/ppermute | solution.py:1561
  196.5 12.5 %copy-start.26 = (bf16[1536,1024]{1,0:T(8,128)(2,1)S(1)}, bf16[1536,1024]{1,0:T(8,128)(2,1)}, u32[]{:S(2)}) copy-start(bf16[1536,1024]{1,0:T(8,128)(2,1)} %copy-done.25) | copy-start | bytes 9437188
  211.3 2.6 copy-start.20
  232.6 1.3 copy-start.5
  233.9 3.2 copy-start.14
  261.2 1.6 copy-start.22
  268.5 13.7 %copy-start.4 = (bf16[1024,1024]{1,0:T(8,128)(2,1)}, bf16[1024,1024]{1,0:T(8,128)(2,1)S(1)}, u32[]{:S(2)}) copy-start(bf16[1024,1024]{1,0:T(8,128)(2,1)S(1)} %convert_element_type.86.g_ref.two_ref) | copy-start | bytes 6291460
  282.3 14.3 %copy-start.13 = (bf16[1024,4096]{1,0:T(8,128)(2,1)}, bf16[1024,4096]{1,0:T(8,128)(2,1)S(1)}, u32[]{:S(2)}) copy-start(bf16[1024,4096]{1,0:T(8,128)(2,1)S(1)} %get-tuple-element.29.pre_ref) | copy-start | bytes 25165828
  282.3 14.3 %copy-start.21 = (bf16[1024,1024]{1,0:T(8,128)(2,1)S(1)}, bf16[1024,1024]{1,0:T(8,128)(2,1)}, u32[]{:S(2)}) copy-start(bf16[1024,1024]{1,0:T(8,128)(2,1)} %copy-done.20) | copy-start | bytes 6291460
  302.2 2.1 copy-start.17
  302.2 0.7 copy-start.7
  302.6 11.3 %collective-permute-start.1 = (bf16[400,1024]{1,0:T(8,128)(2,1)S(1)}, bf16[400,1024]{1,0:T(8,128)(2,1)S(1)}, u32[]{:S(2)}, u32[]{:S(2)}) collective-permute-start(bf16[400,1024]{1,0:T(8,128)(2,1)S(1)} %constant_dynamic-slice_fusion), channel_id=1, source_target_pairs={{0,1},{1,0},{2,3},{3,2},{4,5},{5,4},{6,7},{7,6},{8,9},{9,8},{10,11... | collective-permute-start | bytes 2457608 | tf_op jit(solution)/shard_map/ppermute | solution.py:1584
  306.7 7.6 %copy-start.18 = (f32[1024,1024]{1,0:T(8,128)S(1)}, f32[1024,1024]{1,0:T(8,128)}, u32[]{:S(2)}) copy-start(f32[1024,1024]{1,0:T(8,128)} %copy-done.17) | copy-start | bytes 12582916
  314.8 1.6 copy-start.12
  316.4 3.7 copy-start.24
  316.4 78.6 %slice-start = ((s8[6291456]{0:T(1024)(128)(4,1)}), s8[4194304]{0:T(1024)(128)(4,1)S(1)}, s32[]{:S(2)}) async-start(s8[6291456]{0:T(1024)(128)(4,1)} %bitcast.73), calls=%async_computation.1 | async-start | bytes 8388608
  320.1 74.9 %slice-start.1 = ((s8[6291456]{0:T(1024)(128)(4,1)}), s8[2097152]{0:T(1024)(128)(4,1)S(1)}, s32[]{:S(2)}) async-start(s8[6291456]{0:T(1024)(128)(4,1)} %bitcast.73), calls=%async_computation.2 | async-start | bytes 4194304
  407.8 2.7 copy-start.23
  411.5 203.8 %collective-permute-start.2 = (bf16[400,1024]{1,0:T(8,128)(2,1)}, bf16[400,1024]{1,0:T(8,128)(2,1)S(1)}, u32[]{:S(2)}, u32[]{:S(2)}) collective-permute-start(bf16[400,1024]{1,0:T(8,128)(2,1)} %dynamic-slice_convert_fusion), channel_id=1, source_target_pairs={{0,1},{1,0},{2,3},{3,2},{4,5},{5,4},{6,7},{7,6},{8,9},{9,8},{10,11... | collective-permute-start | bytes 2457608 | tf_op jit(solution)/shard_map/ppermute | solution.py:1591
  412.8 191.3 %copy-start.28 = (f32[12,1024]{1,0:T(8,128)S(1)}, f32[12,1024]{1,0:T(8,128)}, u32[]{:S(2)}) copy-start(f32[12,1024]{1,0:T(8,128)} %param.18) | copy-start | bytes 147460
  412.8 191.3 %copy-start.30 = (f32[12,1024]{1,0:T(8,128)S(1)}, f32[12,1024]{1,0:T(8,128)}, u32[]{:S(2)}) copy-start(f32[12,1024]{1,0:T(8,128)} %param.19) | copy-start | bytes 147460
  412.8 192.9 %copy-start.3 = (f32[1,6,128,1024]{3,2,1,0:T(8,128)S(1)}, f32[1,6,128,1024]{3,2,1,0:T(8,128)}, u32[]{:S(2)}) copy-start(f32[1,6,128,1024]{3,2,1,0:T(8,128)} %param.15) | copy-start | bytes 9437188
  605.7 10.0 %slice-start.2 = ((s8[6291456]{0:T(1024)(128)(4,1)}), s8[4194304]{0:T(1024)(128)(4,1)S(1)}, s32[]{:S(2)}) async-start(s8[6291456]{0:T(1024)(128)(4,1)} %bitcast.82), calls=%async_computation.3 | async-start | bytes 8388608
  605.7 10.0 %copy-start.19 = (f32[1024,1024]{1,0:T(8,128)S(1)}, f32[1024,1024]{1,0:T(8,128)}, u32[]{:S(2)}) copy-start(f32[1024,1024]{1,0:T(8,128)} %copy-done.17) | copy-start | bytes 12582916
  605.7 10.0 %slice-start.3 = ((s8[6291456]{0:T(1024)(128)(4,1)}), s8[2097152]{0:T(1024)(128)(4,1)S(1)}, s32[]{:S(2)}) async-start(s8[6291456]{0:T(1024)(128)(4,1)} %bitcast.82), calls=%async_computation.4 | async-start | bytes 4194304
Sparse Core Ops, SparseCore 0:
  129.3 78.8 all-gather.2
where the time goes:
time: 630 us; the launch traced here: 626 us
  Pallas kernels  454 us (72%)
  matrix products  65 us (10%)
  other arithmetic  38.9 us (6%)
  local copies, waits for them, and re-layouts  29.6 us (5%)
  waiting for transfers between devices  19.3 us (3%)
  between operations  19.1 us (3%)
    pallas_call x1, Pallas kernels, reduce_grads(): pl.pallas_call(reduce_kernel, out_shape=(jax.ShapeDtypeStruct((CAP, 128,...  191 us
    pallas_call x1, Pallas kernels, gather_weights(): pl.pallas_call(gather_kernel, out_shape=tuple((jax.ShapeDtypeStruct((coun...  114 us
    pallas_call x1, Pallas kernels, attend_back(): pl.pallas_call(attn_bwd_kernel, out_shape=jax.ShapeDtypeStruct((3, D, ext...  71.2 us
    dot_general x6, matrix products, mm(): return lax.dot_general(a, b, dims, preferred_element_type=jnp.float32)  65 us
    pallas_call x1, Pallas kernels, attend(): pl.pallas_call(attn_fwd_kernel, out_shape=(jax.ShapeDtypeStruct((D, ext),...  36.1 us
    unnamed x74, local copies, waits for them, and re-layouts  23.1 us
    pallas_call x1, Pallas kernels, feed_up(): pl.pallas_call(up_kernel, out_shape=(out, out), grid=(units // UNITS,), i...  18.7 us
    pallas_call x1, Pallas kernels, feed_down_back(): pl.pallas_call(down_back_kernel, out_shape=(jax.ShapeDtypeStruct((length,...  13.7 us
  transfers between devices with their start and end apart: 4, of which 2 were waited for; matrix products, arithmetic and copies ran while one was open for 7% of the time, Pallas kernels for 39%

commit v1 on v0

--- a/solution.py
+++ b/solution.py
@@ -414,7 +414,7 @@
 
 def attn_bwd_kernel(
     lo_ref, hi_ref, q_ref, k_ref, v_ref, g_ref, c_ref, lse_ref, qaug_ref, kaug_ref, hid_ref,
-    out_ref, kn_ref, vn_ref, acc_ref, dk_acc, dv_acc,
+    out_ref, sums_ref, kn_ref, vn_ref, acc_ref, dk_acc, dv_acc,
 ):
     ext = q_ref.shape[1]
     for h in range(HPG):
@@ -494,6 +494,9 @@
     lax.fori_loop(0, ext // ABLK, query_block, 0)
     out_ref[1] = dk_acc[...].astype(jnp.bfloat16)
     out_ref[2] = dv_acc[...].astype(jnp.bfloat16)
+    for n in range(2):
+        total = jnp.sum(out_ref[2 * n].astype(jnp.float32), axis=1, keepdims=True)
+        sums_ref[n] = jnp.broadcast_to(total, sums_ref.shape[1:])
 
 
 def group_block(offset, rows, ext):
@@ -547,7 +550,10 @@
     rows = HPG * HD
     return pl.pallas_call(
         attn_bwd_kernel,
-        out_shape=jax.ShapeDtypeStruct((3, D, ext), jnp.bfloat16),
+        out_shape=(
+            jax.ShapeDtypeStruct((3, D, ext), jnp.bfloat16),
+            jax.ShapeDtypeStruct((2, D, 128), jnp.float32),
+        ),
         grid_spec=pltpu.PrefetchScalarGridSpec(
             num_scalar_prefetch=2,
             grid=(groups,),
@@ -562,7 +568,10 @@
                 fixed_block(AUG, ext),
                 fixed_block(8, ext),
             ],
-            out_specs=pl.BlockSpec((3, rows, ext), lambda g, lo, hi: (0, g, 0)),
+            out_specs=(
+                pl.BlockSpec((3, rows, ext), lambda g, lo, hi: (0, g, 0)),
+                pl.BlockSpec((2, rows, 128), lambda g, lo, hi: (0, g, 0)),
+            ),
             scratch_shapes=[
                 pltpu.VMEM((HPG, ext, HD + AUG), jnp.bfloat16),
                 pltpu.VMEM((HPG, ext, HD), jnp.bfloat16),
@@ -660,7 +669,7 @@
             pl.BlockSpec((1, UNITS), lambda n: (0, n)),
         ],
         out_specs=(columns, columns),
-        compiler_params=pltpu.CompilerParams(vmem_limit_bytes=40 * 2**20),
+        compiler_params=pltpu.CompilerParams(vmem_limit_bytes=60 * 2**20),
         cost_estimate=pl.CostEstimate(
             flops=2 * length * units * D, bytes_accessed=26 * 10**6, transcendentals=0
         ),
@@ -1054,7 +1063,7 @@
             pltpu.SemaphoreType.DMA,
         ],
         compiler_params=pltpu.CompilerParams(
-            collective_id=1, has_side_effects=True, vmem_limit_bytes=32 * 2**20
+            collective_id=1, has_side_effects=True, vmem_limit_bytes=60 * 2**20
         ),
         cost_estimate=pl.CostEstimate(flops=0, bytes_accessed=50 * 10**6, transcendentals=0),
         name="gather_weights",
@@ -1078,6 +1087,7 @@
             pl.BlockSpec((1, 8, 2, 1, 4, 16, D // 2), lambda m, t: (t, 0, 0, m, 0, 0, 0)),
         ],
         out_specs=pl.BlockSpec((1, 1, 4, 8, 16, D), lambda m, t: (m, t, 0, 0, 0, 0)),
+        compiler_params=pltpu.CompilerParams(vmem_limit_bytes=60 * 2**20),
         cost_estimate=pl.CostEstimate(flops=0, bytes_accessed=17 * 10**6, transcendentals=0),
         name="stack_chunks",
     )(parts)
@@ -1090,8 +1100,9 @@
 
 
 def reduce_kernel(
-    piece_ref, vec_ref, qkv_ref, ctx_ref, pre_ref, hid_ref, tok_ref, gext_ref, norm_ref, two_ref,
-    out_ref, sum_ref,
+    piece_ref, vec_ref, qkv_ref, ctx_ref, pre_ref, hid_ref, tok_ref, gext_ref, norm_ref, two_ref, weight_ref,
+    out_ref, sum_ref, input_ref, border_ref,
+    weight_buf, strip, strip_out, weight_sem, strip_sem, strip_out_sem, border_send, border_recv,
     tile, tall, ext_rhs, row_rhs, far_buf, near_buf, core_in, x_in, y_in, x2_in, y2_in, line, line_in,
     done, parcel, vec_in, vec_out,
     tile_sem, rhs_sem, local_sem, post, mail, send, recv, vec_send, vec_recv,
@@ -1145,6 +1156,50 @@
         def _down():
             body(pltpu.make_async_copy(hid_ref.at[:, columns(8)], tall.at[slot], sem))
 
+    strip_rows = strip.shape[3]
+    strips = qkv_ref.shape[2] // strip_rows
+    weight_copy = pltpu.make_async_copy(weight_ref, weight_buf, weight_sem)
+    weight_copy.start()
+
+    def strip_copy(r):
+        slot = lax.rem(r, 2)
+        here = pl.ds(pl.multiple_of(r * strip_rows, strip_rows), strip_rows)
+        return pltpu.make_async_copy(qkv_ref.at[:, :, here], strip.at[slot], strip_sem.at[slot])
+
+    def strip_done(r):
+        slot = lax.rem(r, 2)
+        here = pl.ds(pl.multiple_of(r * strip_rows, strip_rows), strip_rows)
+        return pltpu.make_async_copy(strip_out.at[slot], input_ref.at[here], strip_out_sem.at[slot])
+
+    def input_strip(r):
+        slot = lax.rem(r, 2)
+
+        @pl.when(r + 1 < strips)
+        def _next():
+            strip_copy(r + 1).start()
+
+        @pl.when(r >= 2)
+        def _free():
+            strip_done(r - 2).wait()
+
+        strip_copy(r).wait()
+        total = mm(strip[slot, 0], weight_buf[0], TN)
+        total += mm(strip[slot, 1], weight_buf[1], TN)
+        total += mm(strip[slot, 2], weight_buf[2], TN)
+        strip_out[slot] = total.astype(jnp.bfloat16)
+        strip_done(r).start()
+
+    halo = border_ref.shape[0]
+    border_at = pl.multiple_of(jnp.where(x == 0, input_ref.shape[0] - EXT_PAD, EXT_PAD - halo), 16)
+    border = pltpu.make_async_remote_copy(
+        src_ref=input_ref.at[pl.ds(border_at, halo)],
+        dst_ref=border_ref,
+        send_sem=border_send,
+        recv_sem=border_recv,
+        device_id=near["x"],
+        device_id_type=MESH,
+    )
+    strip_copy(0).start()
     fetch(0, lambda copy: copy.start())
     greet_all(near, me, n_dp)
 
@@ -1382,6 +1437,20 @@
         def _three():
             stage_three(s - 2 * LAG)
 
+        @pl.when(s == 2)
+        def _weights():
+            weight_copy.wait()
+
+        @pl.when((s >= 2) & (s < 2 + 3 * strips) & (lax.rem(s, 3) == 2))
+        def _input():
+            input_strip(s // 3)
+
+        @pl.when(s == 2 + 3 * strips)
+        def _border():
+            strip_done(strips - 2).wait()
+            strip_done(strips - 1).wait()
+            border.start()
+
         @pl.when(s >= 3 * LAG)
         def _last():
             stage_last(s - 3 * LAG)
@@ -1425,9 +1494,10 @@
     lax.fori_loop(1, n_dp, mail_one, 0)
     for cut in range(SLICES):
         own_letter(cut).wait()
-
-
-def reduce_grads(piece_of, vec, qkv, context, pre, hidden, tokens, ext_grads, normed, two):
+    border.wait()
+
+
+def reduce_grads(piece_of, vec, qkv, context, pre, hidden, tokens, ext_grads, normed, two, weights):
     n_dp = piece_of.shape[0] // CAP
     low = jnp.bfloat16
     width = D // 2 // SLICES
@@ -1441,10 +1511,20 @@
         out_shape=(
             jax.ShapeDtypeStruct((CAP, 128, D), low),
             jax.ShapeDtypeStruct(vec.shape, jnp.float32),
+            jax.ShapeDtypeStruct((ext, D), low),
+            jax.ShapeDtypeStruct((DOC_MAX // 2, D), low),
         ),
-        in_specs=[pl.BlockSpec(memory_space=pltpu.SMEM), vmem] + [anywhere] * 8,
-        out_specs=(anywhere, vmem),
+        in_specs=[pl.BlockSpec(memory_space=pltpu.SMEM), vmem] + [anywhere] * 9,
+        out_specs=(anywhere, vmem, anywhere, anywhere),
         scratch_shapes=[
+            pltpu.VMEM((3, D, D), low),
+            pltpu.VMEM((2, 3, D, 256), low),
+            pltpu.VMEM((2, 256, D), low),
+            pltpu.SemaphoreType.DMA,
+            pltpu.SemaphoreType.DMA((2,)),
+            pltpu.SemaphoreType.DMA((2,)),
+            pltpu.SemaphoreType.DMA,
+            pltpu.SemaphoreType.DMA,
             pltpu.VMEM((2, rows, ext), low),
             pltpu.VMEM((2, length, rows), low),
             pltpu.VMEM((2, 2, SLICES, ext, width), low),
@@ -1476,10 +1556,10 @@
             collective_id=2, has_side_effects=True, vmem_limit_bytes=60 * 2**20
         ),
         cost_estimate=pl.CostEstimate(
-            flops=31 * 10**9, bytes_accessed=50 * 10**6, transcendentals=0
+            flops=41 * 10**9, bytes_accessed=50 * 10**6, transcendentals=0
         ),
         name="reduce_grads",
-    )(piece_of, vec, qkv, context, pre, hidden, tokens, ext_grads, normed, two)
+    )(piece_of, vec, qkv, context, pre, hidden, tokens, ext_grads, normed, two, weights)
 
 
 def coordinates():
@@ -1586,24 +1666,13 @@
     )
     grad_ext = jnp.where(handled[:, None], extend(grad_one_low, halo_grad), 0)
     grad_context = mm(w_out, grad_ext, NT).astype(jnp.bfloat16)
-    grad_qkv = attend_back(lo, hi, qkv, grad_context, context, logs, qaug, kaug, hidden_keys)
-    input_ext = mm(grad_qkv.reshape(3 * D, ext), w_qkv, TN)
-    halo_input = lax.ppermute(halo_part(input_ext).astype(jnp.bfloat16), "tensor", swap)
-    input_back = lax.dynamic_update_slice_in_dim(
-        jnp.zeros((rows, D), jnp.bfloat16), halo_input, edge, 0
-    )
-    input_grad = (grad_one + own_part(input_ext) + input_back.astype(jnp.float32)).astype(
-        jnp.bfloat16
+    grad_qkv, qkv_sums = attend_back(
+        lo, hi, qkv, grad_context, context, logs, qaug, kaug, hidden_keys
     )
 
     vector_terms = jnp.concatenate(
         [
-            jnp.stack(
-                [
-                    jnp.sum(grad_qkv[0].astype(jnp.float32), axis=1),
-                    jnp.sum(grad_qkv[2].astype(jnp.float32), axis=1),
-                ]
-            ),
+            qkv_sums[:, :, 0],
             up_sums.reshape(4, n_tensor, -1)
             .transpose(1, 0, 2)
             .reshape(FF // D, D),
@@ -1623,7 +1692,7 @@
     piece_of = jnp.full((n_dp * CAP,), pieces, jnp.int32).at[slots].set(
         jnp.arange(pieces, dtype=jnp.int32)
     )
-    own_grads, vector_grads = reduce_grads(
+    own_grads, vector_grads, input_ext, halo_input = reduce_grads(
         piece_of,
         vector_terms,
         grad_qkv,
@@ -1634,8 +1703,15 @@
         grad_ext,
         normed_low,
         grad_two_low,
+        w_qkv.reshape(3, D, D),
     )
     own_grads = own_grads.astype(jnp.float32)
+    input_back = lax.dynamic_update_slice_in_dim(
+        jnp.zeros((rows, D), jnp.bfloat16), halo_input, edge, 0
+    )
+    input_grad = (
+        grad_one + own_part(input_ext).astype(jnp.float32) + input_back.astype(jnp.float32)
+    ).astype(jnp.bfloat16)
     slot_new, slot_first_new, slot_second_new = adam_update(
         master_slots[0], slot_first[0], slot_second[0], own_grads, rate_matrix, weight_decay
     )

time: 630 us -> 611 us (0.970)
  local copies, waits for them, and re-layouts: 29.6 us -> 13.9 us
  matrix products: 65 us -> 50.4 us
  waiting for transfers between devices: 19.3 us -> 32.9 us
    unnamed x74 -> x60, local copies, waits for them, and re-layouts: 23.1 us -> 6.01 us
    pallas_call x1, Pallas kernels: 191 us -> 176 us  [reduce_grads(): pl.pallas_call(reduce_kernel, out_shape=(jax.ShapeDtypeStruct((CAP, 128,...]
    dot_general x6 -> x5, matrix products: 65 us -> 50.4 us  [mm(): return lax.dot_general(a, b, dims, preferred_element_type=jnp.float32)]
    ppermute x1, waiting for transfers between devices: 7.12 us -> 15.7 us  [on_device_rows(): lax.ppermute(lax.dynamic_slice_in_dim(grad_one_low, edge, halo, 0), 'tens...]
    pallas_call x1, Pallas kernels: 71.2 us -> 78.9 us  [attend_back(): pl.pallas_call(attn_bwd_kernel, out_shape=(jax.ShapeDtypeStruct((3, D, ex...]
  transfers between devices with their start and end apart: 4 -> 3, of which waited for: 2 -> 2; matrix products, arithmetic and copies ran while one was open for 7% -> 5% of each run, Pallas kernels for 39% -> 10%
where the time goes in v1:
time: 611 us; the launch traced here: 602 us
  Pallas kernels  452 us (74%)
  matrix products  50.4 us (8%)
  other arithmetic  33.6 us (5%)
  waiting for transfers between devices  32.9 us (5%)
  between operations  18.9 us (3%)
  local copies, waits for them, and re-layouts  13.9 us (2%)
    pallas_call x1, Pallas kernels, reduce_grads(): pl.pallas_call(reduce_kernel, out_shape=(jax.ShapeDtypeStruct((CAP, 128,...  176 us
    pallas_call x1, Pallas kernels, gather_weights(): pl.pallas_call(gather_kernel, out_shape=tuple((jax.ShapeDtypeStruct((coun...  115 us
    pallas_call x1, Pallas kernels, attend_back(): pl.pallas_call(attn_bwd_kernel, out_shape=(jax.ShapeDtypeStruct((3, D, ex...  78.9 us
    dot_general x5, matrix products, mm(): return lax.dot_general(a, b, dims, preferred_element_type=jnp.float32)  50.4 us
    pallas_call x1, Pallas kernels, attend(): pl.pallas_call(attn_fwd_kernel, out_shape=(jax.ShapeDtypeStruct((D, ext),...  39.4 us
    pallas_call x1, Pallas kernels, feed_up(): pl.pallas_call(up_kernel, out_shape=(out, out), grid=(units // UNITS,), i...  19.6 us
    ppermute x1, waiting for transfers between devices, on_device_rows(): halo_attn = lax.ppermute(halo_part(attn_ext), 'tensor', swap)  17.1 us
    ppermute x1, waiting for transfers between devices, on_device_rows(): lax.ppermute(lax.dynamic_slice_in_dim(grad_one_low, edge, halo, 0), 'tens...  15.7 us
  transfers between devices with their start and end apart: 3, of which 2 were waited for; matrix products, arithmetic and copies ran while one was open for 5% of the time, Pallas kernels for 10%

profile of v1, /device:TPU:13, one launch (start us, length us, event | category | flops | bytes accessed | tf_op | source)
XLA Modules:
  0.0 601.7 jit_solution(11639926704893303271)
XLA Ops:
  7.3 115.1 %gather_weights.1 = (bf16[3,2,4,128,1024]{4,3,2,1,0:T(8,128)(2,1)}, bf16[1,2,4,128,1024]{4,3,2,1,0:T(8,128)(2,1)}, bf16[4,2,4,128,1024]{4,3,2,1,0:T(8,128)(2,1)}...) custom-call(s32[48]{0:T(128)} %bitcast.100, f32[6,128,1024]{2,1,0:T(8,128)} %bitcast.67, bf16[1024,1024]{1,0:T(8,128)(2,1)} %tokens_ref.1), custom_call_target="tpu_custom_call" | custom-call | bytes 50000000 | tf_op jit(solution)/shard_map/gather_weights/pallas_call | solution.py:1034
  122.7 0.7 select_reduce_fusion.2
  128.1 13.7 %multiply_convert_fusion.q_ref.k_ref.v_ref = bf16[3072,1536]{1,0:T(8,128)(2,1)S(1)} fusion(bf16[3072,1024]{1,0:T(8,128)(2,1)} %bitcast.104, bf16[1536,1024]{1,0:T(8,128)(2,1)} %get-tuple-element.26.tok_ref, f32[3072]{0:T(1024)S(1)} %copy-done.29, f32[3072]{0:T(1024)S(1)} %pad_maximum_fusion), kind=kOutput, calls=%fused_computation.1 | convolution fusion | flops 9677832192 | bytes 18898944 | tf_op jit(solution)/shard_map/dot_general | solution.py:348
  141.8 39.4 %attend.1 = (bf16[1024,1536]{1,0:T(8,128)(2,1)S(1)}, f32[2,8,1536]{2,1,0:T(8,128)S(1)}) custom-call(s32[6]{0:T(128)S(1)} %get-tuple-element.88.lo_ref, s32[6]{0:T(128)S(1)} %get-tuple-element.87.hi_ref, bf16[3072,1536]{1,0:T(8,128)(2,1)S(1)} %multiply_convert_fusion.q_ref.k_ref.v_ref, bf16[3072,1536]{1,0:T(8,128)(2,1)S(1)} %multiply_convert_fusion.q_ref.k_ref.v_ref, ...), custom_call_target="tpu_custom_call" | custom-call | flops 20000000000 | bytes 14000000 | tf_op jit(solution)/shard_map/attend/pallas_call | solution.py:514
  181.2 3.7 convolution_convert_fusion.1
  185.0 1.0 constant_dynamic-slice_fusion.1
  186.0 1.1 copy-done.15
  187.1 0.6 reshape_reshape.6.bias_ref
  187.7 17.1 %collective-permute-done = bf16[400,1024]{1,0:T(8,128)(2,1)S(1)} collective-permute-done((bf16[400,1024]{1,0:T(8,128)(2,1)}, bf16[400,1024]{1,0:T(8,128)(2,1)S(1)}, u32[]{:S(2)}, u32[]{:S(2)}) %collective-permute-start) | collective-permute-done | bytes 819232 | tf_op jit(solution)/shard_map/ppermute | solution.py:1641
  204.8 0.3 broadcast.131.clone
  205.2 2.0 fusion.8
  207.2 1.0 multiply_reduce_fusion.3
  208.3 2.5 fusion.7.x_ref.norm_ref
  210.7 19.6 %feed_up.1 = (bf16[1024,4096]{1,0:T(8,128)(2,1)}, bf16[1024,4096]{1,0:T(8,128)(2,1)}) custom-call(bf16[1024,1024]{1,0:T(8,128)(2,1)} %fusion.7.x_ref.norm_ref, bf16[4096,1024]{1,0:T(8,128)(2,1)} %bitcast.102, f32[1,4096]{1,0:T(1,128)} %reshape_reshape.6.bias_ref), custom_call_target="tpu_custom_call" | custom-call | flops 8589934592 | bytes 26000000 | tf_op jit(solution)/shard_map/feed_up/pallas_call | solution.py:662
  230.3 9.0 %stack_chunks.1 = bf16[4,2,4,8,16,1024]{5,4,3,2,1,0:T(8,128)(2,1)} custom-call(bf16[2,8,2,4,4,16,512]{6,5,4,3,2,1,0:T(8,128)(2,1)} %bitcast.68), custom_call_target="tpu_custom_call" | custom-call | bytes 17000000 | tf_op jit(solution)/shard_map/stack_chunks/pallas_call | solution.py:1082
  239.3 15.0 %fusion.29 = (f32[1024]{0:T(1024)S(1)}, f32[1024,1024]{1,0:T(8,128)S(1)}) fusion(f32[1024]{0:T(1024)S(1)} %bitcast.99, bf16[1024,4096]{1,0:T(8,128)(2,1)} %get-tuple-element.30.hid_ref, bf16[4096,1024]{1,0:T(8,128)(2,1)} %bitcast.69, f32[1024]{0:T(1024)S(1)} %bitcast.96, f32[1024]{0:T(1024)S(1)} %bitcast.83, f32[1024]{0:T(1024)S(1)} %add_rsqrt_fusion.1, ...), kind=kOutput, calls=%fused_computation.109 | convolution fusion | flops 8601467904 | bytes 25194496 | tf_op jit(solution)/shard_map/dot_general | solution.py:348
  254.4 0.6 multiply_reduce_fusion.2
  254.9 1.0 copy-done.11
  255.9 2.3 fusion.6
  258.2 3.4 fusion.24
  261.6 0.3 convert_element_type.78.g_ref.two_ref
  262.0 13.8 %feed_down_back.1 = (bf16[1024,4096]{1,0:T(8,128)(2,1)S(1)}, f32[1,4096]{1,0:T(1,128)S(1)}) custom-call(bf16[1024,1024]{1,0:T(8,128)(2,1)S(1)} %convert_element_type.78.g_ref.two_ref, bf16[4096,1024]{1,0:T(8,128)(2,1)} %bitcast.70, bf16[1024,4096]{1,0:T(8,128)(2,1)} %get-tuple-element.32.slope_ref), custom_call_target="tpu_custom_call" | custom-call | flops 8589934592 | bytes 26000000 | tf_op jit(solution)/shard_map/feed_down_back/pallas_call | solution.py:696
  275.8 14.3 %fusion.30 = f32[1024,1024]{1,0:T(8,128)S(1)} fusion(bf16[1024,4096]{1,0:T(8,128)(2,1)S(1)} %get-tuple-element.33.pre_ref, bf16[4096,1024]{1,0:T(8,128)(2,1)} %bitcast.103), kind=kOutput, calls=%fused_computation.110 | convolution fusion | flops 8589934592 | bytes 20971520 | tf_op jit(solution)/shard_map/dot_general | solution.py:348
  290.1 3.6 multiply_reduce_fusion
  293.7 2.0 fusion.26
  295.8 1.9 copy-done.6
  297.7 0.3 convert_element_type.80
  298.1 0.3 collective-permute-start.1
  298.6 1.2 scatter_custom_fusion.piece_ref
  299.9 0.5 broadcast.182
  300.4 0.7 reduce.5
  301.1 15.7 %collective-permute-done.1 = bf16[400,1024]{1,0:T(8,128)(2,1)S(1)} collective-permute-done((bf16[400,1024]{1,0:T(8,128)(2,1)S(1)}, bf16[400,1024]{1,0:T(8,128)(2,1)S(1)}, u32[]{:S(2)}, u32[]{:S(2)}) %collective-permute-start.1) | collective-permute-done | bytes 819232 | tf_op jit(solution)/shard_map/ppermute | solution.py:1664
  316.9 0.4 broadcast_in_dim.151
  317.3 0.4 constant_dynamic-update-slice_fusion.1
  317.8 1.1 broadcast_select_fusion.gext_ref
  318.9 0.5 copy-done.28
  319.4 3.7 convolution_convert_fusion.g_ref
  323.1 78.9 %attend_back.1 = (bf16[3,1024,1536]{2,1,0:T(8,128)(2,1)}, f32[2,1024,128]{2,1,0:T(8,128)S(1)}) custom-call(s32[6]{0:T(128)S(1)} %get-tuple-element.88.lo_ref, s32[6]{0:T(128)S(1)} %get-tuple-element.87.hi_ref, bf16[3072,1536]{1,0:T(8,128)(2,1)} %copy-done.3, bf16[3072,1536]{1,0:T(8,128)(2,1)} %copy-done.3, bf16[3072,1536]{1,0:T(8,128)(2,1)} %copy-done.3, ...), custom_call_target="tpu_custom_call" | custom-call | flops 49999998976 | bytes 30000000 | tf_op jit(solution)/shard_map/attend_back/pallas_call | solution.py:551
  402.0 0.6 copy.26
  402.6 1.3 concatenate.15.vec_ref
  403.9 176.0 %reduce_grads.1 = (bf16[6,128,1024]{2,1,0:T(8,128)(2,1)}, f32[12,1024]{1,0:T(8,128)}, bf16[1536,1024]{1,0:T(8,128)(2,1)}, bf16[400,1024]{1,0:T(8,128)(2,1)}) custom-call(s32[96]{0:T(128)} %scatter_custom_fusion.piece_ref, f32[12,1024]{1,0:T(8,128)} %concatenate.15.vec_ref, bf16[3,1024,1536]{2,1,0:T(8,128)(2,1)} %get-tuple-element.37.qkv_ref, ...), custom_call_target="tpu_custom_call" | custom-call | flops 41000001536 | bytes 50000000 | tf_op jit(solution)/shard_map/reduce_grads/pallas_call | solution.py:1509
  579.9 0.3 broadcast.131
  580.1 1.4 constant_dynamic-update-slice_fusion
  581.5 0.5 copy-done.18
  582.0 5.0 add_convert_fusion
  587.0 0.9 copy-done.13
  587.9 6.1 %fusion.11 = (f32[1,6,128,1024]{3,2,1,0:T(8,128)}, f32[1,6,128,1024]{3,2,1,0:T(8,128)}, f32[1,6,128,1024]{3,2,1,0:T(8,128)}) fusion(bf16[6,128,1024]{2,1,0:T(8,128)(2,1)S(1)} %copy-done.17, f32[1,6,128,1024]{3,2,1,0:T(8,128)S(1)} %copy-done.12, f32[1,6,128,1024]{3,2,1,0:T(8,128)S(1)} %copy-done.13, f32[1,6,128,1024]{3,2,1,0:T(8,128)S(1)} %copy-done.10), kind=kLoop, calls=%fused_computation.36 | loop fusion | flops 11796480 | bytes 20447232 | tf_op jit(solution)/shard_map/broadcast_in_dim | solution.py:1726
  594.0 0.7 multiply_subtract_fusion
  (101 shorter events, 1.8 us)
Async XLA Ops:
  7.2 120.9 %copy-start.29 = (f32[3072]{0:T(1024)S(1)}, f32[3072]{0:T(1024)}, u32[]{:S(2)}) copy-start(f32[3072]{0:T(1024)} %constant.94.clone.1) | copy-start | bytes 36868
  7.2 115.2 %copy-start.21 = (s32[1,2048]{1,0:T(1,128)S(1)}, s32[1,2048]{1,0:T(1,128)}, u32[]{:S(2)}) copy-start(s32[1,2048]{1,0:T(1,128)} %param.12) | copy-start | bytes 24580
  7.2 120.6 %copy-start.25 = (s32[1,2048]{1,0:T(1,128)S(1)}, s32[1,2048]{1,0:T(1,128)}, u32[]{:S(2)}) copy-start(s32[1,2048]{1,0:T(1,128)} %param.13) | copy-start | bytes 24580
  7.2 120.7 %copy-start.19 = (f32[12,1024]{1,0:T(8,128)S(1)}, f32[12,1024]{1,0:T(8,128)}, u32[]{:S(2)}) copy-start(f32[12,1024]{1,0:T(8,128)} %param.18) | copy-start | bytes 147460
  7.2 223.1 %all-gather.3.cloned.1.call-start = ((), (), s32[]{:S(2)}) async-start(), calls=%async_computation | async-start | bytes 8650752 | tf_op jit(solution)/shard_map/all_gather | solution.py:1630
  141.8 39.4 %copy-start.3 = (bf16[3072,1536]{1,0:T(8,128)(2,1)}, bf16[3072,1536]{1,0:T(8,128)(2,1)S(1)}, u32[]{:S(2)}) copy-start(bf16[3072,1536]{1,0:T(8,128)(2,1)S(1)} %multiply_convert_fusion.q_ref.k_ref.v_ref) | copy-start | bytes 28311556
  141.8 39.4 %copy-start.27 = (bf16[1,2,4,128,1024]{4,3,2,1,0:T(8,128)(2,1)S(1)}, bf16[1,2,4,128,1024]{4,3,2,1,0:T(8,128)(2,1)}, u32[]{:S(2)}) copy-start(bf16[1,2,4,128,1024]{4,3,2,1,0:T(8,128)(2,1)} %get-tuple-element.28) | copy-start | bytes 6291460
  181.2 3.8 copy-start.2
  185.0 2.0 copy-start.15
  185.0 20.2 %copy-start.4 = (bf16[1024,1024]{1,0:T(8,128)(2,1)S(1)}, bf16[1024,1024]{1,0:T(8,128)(2,1)}, u32[]{:S(2)}) copy-start(bf16[1024,1024]{1,0:T(8,128)(2,1)} %tokens_ref.1) | copy-start | bytes 6291460
  187.0 17.8 %collective-permute-start = (bf16[400,1024]{1,0:T(8,128)(2,1)}, bf16[400,1024]{1,0:T(8,128)(2,1)S(1)}, u32[]{:S(2)}, u32[]{:S(2)}) collective-permute-start(bf16[400,1024]{1,0:T(8,128)(2,1)} %constant_dynamic-slice_fusion.1), channel_id=1, source_target_pairs={{0,1},{1,0},{2,3},{3,2},{4,5},{5,4},{6,7},{7,6},{8,9},{9,8},{10,11... | collective-permute-start | bytes 2457608 | tf_op jit(solution)/shard_map/ppermute | solution.py:1641
  187.7 17.5 %copy-start.16 = (bf16[1536,1024]{1,0:T(8,128)(2,1)S(1)}, bf16[1536,1024]{1,0:T(8,128)(2,1)}, u32[]{:S(2)}) copy-start(bf16[1536,1024]{1,0:T(8,128)(2,1)} %copy-done.15) | copy-start | bytes 9437188
  207.2 3.5 copy-start.8
  254.3 1.6 copy-start.11
  261.9 13.8 %copy-start = (bf16[1024,1024]{1,0:T(8,128)(2,1)}, bf16[1024,1024]{1,0:T(8,128)(2,1)S(1)}, u32[]{:S(2)}) copy-start(bf16[1024,1024]{1,0:T(8,128)(2,1)S(1)} %convert_element_type.78.g_ref.two_ref) | copy-start | bytes 6291460
  275.7 14.3 %copy-start.1 = (bf16[1024,4096]{1,0:T(8,128)(2,1)}, bf16[1024,4096]{1,0:T(8,128)(2,1)S(1)}, u32[]{:S(2)}) copy-start(bf16[1024,4096]{1,0:T(8,128)(2,1)S(1)} %get-tuple-element.33.pre_ref) | copy-start | bytes 25165828
  275.8 14.3 %copy-start.5 = (bf16[1024,1024]{1,0:T(8,128)(2,1)S(1)}, bf16[1024,1024]{1,0:T(8,128)(2,1)}, u32[]{:S(2)}) copy-start(bf16[1024,1024]{1,0:T(8,128)(2,1)} %tokens_ref.1) | copy-start | bytes 6291460
  275.8 14.3 %copy-start.9 = (bf16[1024,1024]{1,0:T(8,128)(2,1)S(1)}, bf16[1024,1024]{1,0:T(8,128)(2,1)}, u32[]{:S(2)}) copy-start(bf16[1024,1024]{1,0:T(8,128)(2,1)} %copy-done.8) | copy-start | bytes 6291460
  295.8 2.0 copy-start.6
  295.8 2.7 copy-start.26
  298.1 18.8 %collective-permute-start.1 = (bf16[400,1024]{1,0:T(8,128)(2,1)S(1)}, bf16[400,1024]{1,0:T(8,128)(2,1)S(1)}, u32[]{:S(2)}, u32[]{:S(2)}) collective-permute-start(bf16[400,1024]{1,0:T(8,128)(2,1)S(1)} %constant_dynamic-slice_fusion), channel_id=1, source_target_pairs={{0,1},{1,0},{2,3},{3,2},{4,5},{5,4},{6,7},{7,6},{8,9},{9,8},{10,11... | collective-permute-start | bytes 2457608 | tf_op jit(solution)/shard_map/ppermute | solution.py:1664
  301.1 16.2 %copy-start.7 = (f32[1024,1024]{1,0:T(8,128)S(1)}, f32[1024,1024]{1,0:T(8,128)}, u32[]{:S(2)}) copy-start(f32[1024,1024]{1,0:T(8,128)} %copy-done.6) | copy-start | bytes 12582916
  317.8 1.6 copy-start.28
  319.4 3.7 copy-start.14
  579.9 2.1 copy-start.18
  580.1 6.8 %copy-start.17 = (bf16[6,128,1024]{2,1,0:T(8,128)(2,1)S(1)}, bf16[6,128,1024]{2,1,0:T(8,128)(2,1)}, u32[]{:S(2)}) copy-start(bf16[6,128,1024]{2,1,0:T(8,128)(2,1)} %get-tuple-element.40) | copy-start | bytes 4718596
  582.0 5.0 copy-start.10
  582.0 5.0 copy-start.12
  582.0 5.9 copy-start.13
  587.9 6.1 %copy-start.20 = (f32[12,1024]{1,0:T(8,128)S(1)}, f32[12,1024]{1,0:T(8,128)}, u32[]{:S(2)}) copy-start(f32[12,1024]{1,0:T(8,128)} %param.18) | copy-start | bytes 147460
  587.9 6.1 %copy-start.22 = (f32[12,1024]{1,0:T(8,128)S(1)}, f32[12,1024]{1,0:T(8,128)}, u32[]{:S(2)}) copy-start(f32[12,1024]{1,0:T(8,128)} %param.19) | copy-start | bytes 147460
  587.9 6.1 %copy-start.23 = (f32[12,1024]{1,0:T(8,128)S(1)}, f32[12,1024]{1,0:T(8,128)}, u32[]{:S(2)}) copy-start(f32[12,1024]{1,0:T(8,128)} %param.20) | copy-start | bytes 147460
  587.9 6.1 %copy-start.24 = (f32[12,1024]{1,0:T(8,128)S(1)}, f32[12,1024]{1,0:T(8,128)}, u32[]{:S(2)}) copy-start(f32[12,1024]{1,0:T(8,128)} %get-tuple-element.41) | copy-start | bytes 147460
Sparse Core Ops, SparseCore 0:
  122.5 84.4 all-gather.2

commit v2 on v1

--- a/solution.py
+++ b/solution.py
@@ -333,7 +333,6 @@
 
 
 DOC_MAX = 800
-EXT_PAD = 512
 ABLK = 256
 FINE = 128
 HPG = 8
@@ -580,7 +579,7 @@
                 pltpu.VMEM((rows, ext), jnp.float32),
             ],
         ),
-        compiler_params=pltpu.CompilerParams(vmem_limit_bytes=48 * 2**20),
+        compiler_params=pltpu.CompilerParams(vmem_limit_bytes=56 * 2**20),
         cost_estimate=pl.CostEstimate(flops=50 * 10**9, bytes_accessed=30 * 10**6, transcendentals=0),
         name="attend_back",
     )(lo, hi, qkv, qkv, qkv, grads, context, logs, qaug, kaug, hidden)
@@ -588,40 +587,21 @@
 
 def document_plan(segment, valid, half, rows):
     length = segment.shape[0]
-    ext = rows + EXT_PAD
-    base = half * EXT_PAD
     position = jnp.arange(length, dtype=jnp.int32)
     documents = jnp.arange(8, dtype=jnp.int32)[:, None]
-    one_hot = segment[None, :] == documents
-    counts = jnp.sum(one_hot.astype(jnp.int32), axis=1, keepdims=True)
+    hot = segment[None, :] == documents
+    counts = jnp.sum(hot.astype(jnp.int32), axis=1, keepdims=True)
     starts = jnp.sum((segment[None, :] < documents).astype(jnp.int32), axis=1, keepdims=True)
-    start = jnp.sum(jnp.where(one_hot, starts, 0), axis=0)
-    end = jnp.sum(jnp.where(one_hot, starts + counts, 0), axis=0)
-    crossing = (start < rows) & (end > rows)
-    left = jnp.max(jnp.where(crossing, rows - start, 0))
-    right = jnp.max(jnp.where(crossing, end - rows, 0))
-    in_left = position < rows
-    work = jnp.where(crossing, 0, end - start)
-    left_work = jnp.sum(jnp.where(in_left, work, 0))
-    right_work = jnp.sum(jnp.where(in_left, 0, work))
-    both_fit = (left <= DOC_MAX // 2) & (right <= DOC_MAX // 2)
-    second = jnp.where(both_fit, right_work <= left_work, left <= right)
-    worker = jnp.where(second, half == 1, half == 0)
+    start = jnp.sum(jnp.where(hot, starts, 0), axis=0)
+    end = jnp.sum(jnp.where(hot, starts + counts, 0), axis=0)
     own = (position >= half * rows) & (position < (half + 1) * rows)
-    handled = jnp.where(crossing, worker, own)
-    cut = lambda values: lax.dynamic_slice_in_dim(values, base, ext, 0)
-    handled_ext = cut(handled)
-    begins = jnp.where(handled_ext, cut(start) - base, ext).reshape(-1, ABLK)
-    ends = jnp.where(handled_ext, cut(end) - base, 0).reshape(-1, ABLK)
-    lo = jnp.min(begins, axis=1) // FINE
+    begins = jnp.where(own, start, length).reshape(-1, ABLK)
+    ends = jnp.where(own, end, 0).reshape(-1, ABLK)
     hi = (jnp.max(ends, axis=1) + (FINE - 1)) // FINE
-    blank = jnp.max(ends, axis=1) == 0
-    lo = jnp.where(blank, 0, lo)
-    hi = jnp.where(blank, 0, hi)
-    hot = cut(one_hot.T).T
-    masked = cut(valid) == 0
-    ones = jnp.ones((1, ext), jnp.bfloat16)
-    fill = jnp.zeros((AUG - 9, ext), jnp.bfloat16)
+    lo = jnp.where(hi == 0, 0, jnp.min(begins, axis=1) // FINE)
+    masked = valid == 0
+    ones = jnp.ones((1, length), jnp.bfloat16)
+    fill = jnp.zeros((AUG - 9, length), jnp.bfloat16)
     qaug = jnp.concatenate([hot.astype(jnp.bfloat16), ones, fill], axis=0)
     kaug = jnp.concatenate(
         [
@@ -631,9 +611,8 @@
         ],
         axis=0,
     )
-    hidden = jnp.broadcast_to(masked.astype(jnp.float32)[None, :], (8, ext))
-    foreign = lax.dynamic_slice_in_dim(crossing & ~worker, half * rows, rows, 0)
-    return lo, hi, qaug, kaug, hidden, handled_ext, foreign
+    hidden = jnp.broadcast_to(masked.astype(jnp.float32)[None, :], (8, length))
+    return lo, hi, qaug, kaug, hidden
 
 
 def normal_parts(values):
@@ -808,11 +787,11 @@
     lax.fori_loop(1, n_dp, post_one, 0)
 
     rows = tokens_ref.shape[0]
-    halo = DOC_MAX // 2
+    halo = DOC_MAX
     blank = zero_ref.shape[0]
     zero_ref[...] = jnp.zeros_like(zero_ref)
     edge = pl.multiple_of(jnp.where(x == 0, rows - halo, 0), 16)
-    there = pl.multiple_of(jnp.where(x == 0, EXT_PAD - halo, rows), 16)
+    there = pl.multiple_of(jnp.where(x == 0, rows - halo, rows), 16)
     rest = pl.multiple_of(jnp.where(x == 0, rows + halo, 0), 16)
     border = pltpu.make_async_remote_copy(
         src_ref=tokens_ref.at[pl.ds(edge, halo)],
@@ -824,7 +803,7 @@
     )
     border.start()
     inside = pltpu.make_async_copy(
-        tokens_ref, ext_ref.at[pl.ds(pl.multiple_of(x * EXT_PAD, 16), rows)], ext_sem.at[0]
+        tokens_ref, ext_ref.at[pl.ds(pl.multiple_of(x * rows, 16), rows)], ext_sem.at[0]
     )
     inside.start()
     empty = pltpu.make_async_copy(zero_ref, ext_ref.at[pl.ds(rest, blank)], ext_sem.at[1])
@@ -1038,7 +1017,7 @@
         )
         + (
             jax.ShapeDtypeStruct((4, 4, 16, D // 2), low),
-            jax.ShapeDtypeStruct((rows + EXT_PAD, D), tokens.dtype),
+            jax.ShapeDtypeStruct((2 * rows, D), tokens.dtype),
         ),
         in_specs=[
             pl.BlockSpec(memory_space=pltpu.SMEM),
@@ -1051,7 +1030,7 @@
             pltpu.VMEM((n_dp, CAP, 16, D // 2), low),
             pltpu.VMEM((n_dp * CAP, 16, D // 2), low),
             pltpu.VMEM((12, 4, 16, D // 2), low),
-            pltpu.VMEM((EXT_PAD - DOC_MAX // 2, D), tokens.dtype),
+            pltpu.VMEM((rows - DOC_MAX, D), tokens.dtype),
             pltpu.SemaphoreType.DMA,
             pltpu.SemaphoreType.DMA((CHUNKS,)),
             pltpu.SemaphoreType.DMA((2,)),
@@ -1133,16 +1112,22 @@
         part = pl.ds(pl.multiple_of(lax.rem(n, tiles) * rows, rows), rows)
         slot = lax.rem(n, 2)
         ext = ext_rhs.shape[3]
-        wide = tile.at[slot, :, pl.ds(0, ext)]
+        wide = tile.at[slot]
+        near_half = tile.at[slot, :, pl.ds(0, ext // 2)]
+        own = pl.ds(pl.multiple_of(x * (ext // 2), 128), ext // 2)
         sem = tile_sem.at[slot]
 
-        @pl.when(i < 3)
-        def _qkv():
+        @pl.when(i == 0)
+        def _q():
+            body(pltpu.make_async_copy(qkv_ref.at[0, part, own], near_half, sem))
+
+        @pl.when((i == 1) | (i == 2))
+        def _kv():
             body(pltpu.make_async_copy(qkv_ref.at[i, part, :], wide, sem))
 
         @pl.when(i == 3)
         def _out():
-            body(pltpu.make_async_copy(ctx_ref.at[part, :], wide, sem))
+            body(pltpu.make_async_copy(ctx_ref.at[part, own], near_half, sem))
 
         def columns(first):
             start = (i - first) * 1024 + lax.rem(n, tiles) * rows
@@ -1161,14 +1146,18 @@
     weight_copy = pltpu.make_async_copy(weight_ref, weight_buf, weight_sem)
     weight_copy.start()
 
+    def strip_at(r):
+        other = lax.rem(r + (1 - x) * (strips // 2), strips)
+        return pl.ds(pl.multiple_of(other * strip_rows, strip_rows), strip_rows)
+
     def strip_copy(r):
         slot = lax.rem(r, 2)
-        here = pl.ds(pl.multiple_of(r * strip_rows, strip_rows), strip_rows)
+        here = strip_at(r)
         return pltpu.make_async_copy(qkv_ref.at[:, :, here], strip.at[slot], strip_sem.at[slot])
 
     def strip_done(r):
         slot = lax.rem(r, 2)
-        here = pl.ds(pl.multiple_of(r * strip_rows, strip_rows), strip_rows)
+        here = strip_at(r)
         return pltpu.make_async_copy(strip_out.at[slot], input_ref.at[here], strip_out_sem.at[slot])
 
     def input_strip(r):
@@ -1183,14 +1172,26 @@
             strip_done(r - 2).wait()
 
         strip_copy(r).wait()
-        total = mm(strip[slot, 0], weight_buf[0], TN)
-        total += mm(strip[slot, 1], weight_buf[1], TN)
-        total += mm(strip[slot, 2], weight_buf[2], TN)
-        strip_out[slot] = total.astype(jnp.bfloat16)
+        mine = lax.rem(r + (1 - x) * (strips // 2), strips) // (strips // 2) == x
+
+        @pl.when(mine)
+        def _own():
+            total = mm(strip[slot, 0], weight_buf[0], TN)
+            total += mm(strip[slot, 1], weight_buf[1], TN)
+            total += mm(strip[slot, 2], weight_buf[2], TN)
+            strip_out[slot] = total.astype(jnp.bfloat16)
+
+        @pl.when(jnp.logical_not(mine))
+        def _other():
+            total = mm(strip[slot, 1], weight_buf[1], TN)
+            total += mm(strip[slot, 2], weight_buf[2], TN)
+            strip_out[slot] = total.astype(jnp.bfloat16)
+
         strip_done(r).start()
 
     halo = border_ref.shape[0]
-    border_at = pl.multiple_of(jnp.where(x == 0, input_ref.shape[0] - EXT_PAD, EXT_PAD - halo), 16)
+    middle = input_ref.shape[0] // 2
+    border_at = pl.multiple_of(jnp.where(x == 0, middle, middle - halo), 16)
     border = pltpu.make_async_remote_copy(
         src_ref=input_ref.at[pl.ds(border_at, halo)],
         dst_ref=border_ref,
@@ -1279,11 +1280,19 @@
             def put(value, to):
                 to[ring, t, pl.ds(p, 2)] = value.astype(jnp.bfloat16).reshape(2, 4, 2, 16, width)
 
-            @pl.when(i < 4)
+            @pl.when((i == 1) | (i == 2))
             def _wide():
-                which = jnp.where(i < 3, 0, 1)
-                put(mm(tile[slot], ext_rhs[which, 0, cut], NN), far_buf)
-                put(mm(tile[slot], ext_rhs[which, 1, cut], NN), near_buf)
+                put(mm(tile[slot], ext_rhs[0, 0, cut], NN), far_buf)
+                put(mm(tile[slot], ext_rhs[0, 1, cut], NN), near_buf)
+
+            @pl.when((i == 0) | (i == 3))
+            def _own():
+                which = jnp.where(i == 0, 0, 1)
+                length = ext_rhs.shape[3] // 2
+                own = pl.ds(pl.multiple_of(x * length, length), length)
+                left = tile[slot, :, 0:length]
+                put(mm(left, ext_rhs[which, 0, cut, own], NN), far_buf)
+                put(mm(left, ext_rhs[which, 1, cut, own], NN), near_buf)
 
             @pl.when(i >= 4)
             def _tall():
@@ -1445,7 +1454,7 @@
         def _input():
             input_strip(s // 3)
 
-        @pl.when(s == 2 + 3 * strips)
+        @pl.when(s == STEPS + LAG)
         def _border():
             strip_done(strips - 2).wait()
             strip_done(strips - 1).wait()
@@ -1512,7 +1521,7 @@
             jax.ShapeDtypeStruct((CAP, 128, D), low),
             jax.ShapeDtypeStruct(vec.shape, jnp.float32),
             jax.ShapeDtypeStruct((ext, D), low),
-            jax.ShapeDtypeStruct((DOC_MAX // 2, D), low),
+            jax.ShapeDtypeStruct((DOC_MAX, D), low),
         ),
         in_specs=[pl.BlockSpec(memory_space=pltpu.SMEM), vmem] + [anywhere] * 9,
         out_specs=(anywhere, vmem, anywhere, anywhere),
@@ -1553,7 +1562,7 @@
             pltpu.SemaphoreType.DMA((5,)),
         ],
         compiler_params=pltpu.CompilerParams(
-            collective_id=2, has_side_effects=True, vmem_limit_bytes=60 * 2**20
+            collective_id=2, has_side_effects=True, vmem_limit_bytes=63 * 2**20
         ),
         cost_estimate=pl.CostEstimate(
             flops=41 * 10**9, bytes_accessed=50 * 10**6, transcendentals=0
@@ -1596,27 +1605,9 @@
     half = lax.axis_index("tensor")
     every = ("tensor", "dp")
     rows = tokens.shape[0]
-    ext = rows + EXT_PAD
-    halo = DOC_MAX // 2
-    swap = [(0, 1), (1, 0)]
-    edge = jnp.where(half == 0, rows - halo, 0)
-    halo_at = jnp.where(half == 0, rows, EXT_PAD - halo)
-    own_at = half * EXT_PAD
-
-    def extend(own_rows, halo_rows):
-        whole = jnp.zeros((ext,) + own_rows.shape[1:], own_rows.dtype)
-        whole = lax.dynamic_update_slice_in_dim(whole, halo_rows, halo_at, 0)
-        return lax.dynamic_update_slice_in_dim(whole, own_rows, own_at, 0)
-
-    def own_part(values):
-        return lax.dynamic_slice_in_dim(values, own_at, rows, 0)
-
-    def halo_part(values):
-        return lax.dynamic_slice_in_dim(values, halo_at, halo, 0)
-
-    lo, hi, qaug, kaug, hidden_keys, handled, foreign = document_plan(
-        segment_ids[0], key_mask[0], half, rows
-    )
+    ext = 2 * rows
+    own_at = half * rows
+    lo, hi, qaug, kaug, hidden_keys = document_plan(segment_ids[0], key_mask[0], half, rows)
     slots = slot_index(owners)
     pieces = slots.shape[0]
     piece_rows = master_slots.shape[2]
@@ -1637,12 +1628,8 @@
         (mm(w_qkv, tokens_ext, NT) + bias_qkv[:, None]) * scale_qkv.astype(jnp.float32)[:, None]
     ).astype(jnp.bfloat16)
     context, logs = attend(lo, hi, qkv, qaug, kaug, hidden_keys)
-    attn_ext = mm(context, w_out, TN).astype(jnp.bfloat16)
-    halo_attn = lax.ppermute(halo_part(attn_ext), "tensor", swap)
-    attn_back = lax.dynamic_update_slice_in_dim(
-        jnp.zeros((rows, D), jnp.bfloat16), halo_attn, edge, 0
-    )
-    attn_sum = jnp.where(foreign[:, None], attn_back, own_part(attn_ext)).astype(jnp.float32)
+    own_context = lax.dynamic_slice_in_dim(context, own_at, rows, 1)
+    attn_sum = mm(own_context, w_out, TN).astype(jnp.bfloat16).astype(jnp.float32)
     residual_one = tokens.astype(jnp.float32) + (attn_sum + vectors[6])
     normal_one, inverse_one = layer_stats(residual_one)
     normed = normal_one * vectors[8] + vectors[9]
@@ -1661,11 +1648,15 @@
     grad_one = norm_back(grad_norm, normal_one, inverse_one, vectors[8])
     grad_one_low = grad_one.astype(jnp.bfloat16)
 
-    halo_grad = lax.ppermute(
-        lax.dynamic_slice_in_dim(grad_one_low, edge, halo, 0), "tensor", swap
-    )
-    grad_ext = jnp.where(handled[:, None], extend(grad_one_low, halo_grad), 0)
-    grad_context = mm(w_out, grad_ext, NT).astype(jnp.bfloat16)
+    grad_ext = lax.dynamic_update_slice_in_dim(
+        jnp.zeros((ext, D), jnp.bfloat16), grad_one_low, own_at, 0
+    )
+    grad_context = lax.dynamic_update_slice_in_dim(
+        jnp.zeros((D, ext), jnp.bfloat16),
+        mm(w_out, grad_one_low, NT).astype(jnp.bfloat16),
+        own_at,
+        1,
+    )
     grad_qkv, qkv_sums = attend_back(
         lo, hi, qkv, grad_context, context, logs, qaug, kaug, hidden_keys
     )
@@ -1707,10 +1698,13 @@
     )
     own_grads = own_grads.astype(jnp.float32)
     input_back = lax.dynamic_update_slice_in_dim(
-        jnp.zeros((rows, D), jnp.bfloat16), halo_input, edge, 0
+        jnp.zeros((rows, D), jnp.bfloat16),
+        halo_input,
+        jnp.where(half == 0, rows - DOC_MAX, 0),
+        0,
     )
     input_grad = (
-        grad_one + own_part(input_ext).astype(jnp.float32) + input_back.astype(jnp.float32)
+        grad_one + lax.dynamic_slice_in_dim(input_ext, own_at, rows, 0).astype(jnp.float32) + input_back.astype(jnp.float32)
     ).astype(jnp.bfloat16)
     slot_new, slot_first_new, slot_second_new = adam_update(
         master_slots[0], slot_first[0], slot_second[0], own_grads, rate_matrix, weight_decay

time: 611 us -> 568 us (0.930)
  waiting for transfers between devices: 32.9 us -> 0.02 us
  Pallas kernels: 452 us -> 442 us
    ppermute x2 -> x0, waiting for transfers between devices: 32.9 us -> none  [the longest x1 17.1 us: on_device_rows(): halo_attn = lax.ppermute(halo_part(attn_ext), 'tensor', swap)]
    pallas_call x1, Pallas kernels: 78.9 us -> 62.2 us  [attend_back(): pl.pallas_call(attn_bwd_kernel, out_shape=(jax.ShapeDtypeStruct((3, D, ex...]
    pallas_call x1, Pallas kernels: 176 us -> 190 us  [reduce_grads(): pl.pallas_call(reduce_kernel, out_shape=(jax.ShapeDtypeStruct((CAP, 128,...]
    pallas_call x1, Pallas kernels: 39.4 us -> 32.2 us  [attend(): pl.pallas_call(attn_fwd_kernel, out_shape=(jax.ShapeDtypeStruct((D, ext),...]
  transfers between devices with their start and end apart: 3 -> 1, of which waited for: 2 -> 0; matrix products, arithmetic and copies ran while one was open for 5% -> 5% of each run, Pallas kernels for 10% -> 9%
where the time goes in v2:
time: 568 us; the launch traced here: 560 us
  Pallas kernels  442 us (78%)
  matrix products  54.7 us (10%)
  other arithmetic  31.5 us (6%)
  local copies, waits for them, and re-layouts  16.9 us (3%)
  between operations  14.9 us (3%)
    pallas_call x1, Pallas kernels, reduce_grads(): pl.pallas_call(reduce_kernel, out_shape=(jax.ShapeDtypeStruct((CAP, 128,...  190 us
    pallas_call x1, Pallas kernels, gather_weights(): pl.pallas_call(gather_kernel, out_shape=tuple((jax.ShapeDtypeStruct((coun...  115 us
    pallas_call x1, Pallas kernels, attend_back(): pl.pallas_call(attn_bwd_kernel, out_shape=(jax.ShapeDtypeStruct((3, D, ex...  62.2 us
    dot_general x5, matrix products, mm(): return lax.dot_general(a, b, dims, preferred_element_type=jnp.float32)  54.7 us
    pallas_call x1, Pallas kernels, attend(): pl.pallas_call(attn_fwd_kernel, out_shape=(jax.ShapeDtypeStruct((D, ext),...  32.2 us
    pallas_call x1, Pallas kernels, feed_up(): pl.pallas_call(up_kernel, out_shape=(out, out), grid=(units // UNITS,), i...  19.5 us
    pallas_call x1, Pallas kernels, feed_down_back(): pl.pallas_call(down_back_kernel, out_shape=(jax.ShapeDtypeStruct((length,...  13.7 us
  transfers between devices with their start and end apart: 1, of which 0 were waited for; matrix products, arithmetic and copies ran while one was open for 5% of the time, Pallas kernels for 9%

profile of v2, /device:TPU:13, one launch (start us, length us, event | category | flops | bytes accessed | tf_op | source)
XLA Modules:
  0.0 559.9 jit_solution(9818404859491716275)
XLA Ops:
  7.2 0.0 all-gather.3.cloned.1.call-start
  7.3 115.1 %gather_weights.1 = (bf16[3,2,4,128,1024]{4,3,2,1,0:T(8,128)(2,1)}, bf16[1,2,4,128,1024]{4,3,2,1,0:T(8,128)(2,1)}, bf16[4,2,4,128,1024]{4,3,2,1,0:T(8,128)(2,1)}...) custom-call(s32[48]{0:T(128)} %bitcast.101, f32[6,128,1024]{2,1,0:T(8,128)} %bitcast.66, bf16[1024,1024]{1,0:T(8,128)(2,1)} %tokens_ref.1), custom_call_target="tpu_custom_call" | custom-call | bytes 50000000 | tf_op jit(solution)/shard_map/gather_weights/pallas_call | solution.py:1013
  122.4 0.2 convert_reduce_fusion.1
  122.6 0.1 select_reduce_fusion
  122.7 0.1 pad.5.clone
  122.8 0.1 pad.4.clone
  122.9 0.6 reshape_reshape.6.bias_ref
  123.6 0.2 convert_reduce_fusion.3
  123.7 1.2 scatter_custom_fusion.piece_ref
  125.0 0.2 select_reduce_fusion.2
  125.3 0.1 maximum_maximum_fusion.1
  125.4 20.4 %multiply_convert_fusion.q_ref.k_ref.v_ref = bf16[3072,2048]{1,0:T(8,128)(2,1)} fusion(bf16[3072,1024]{1,0:T(8,128)(2,1)} %bitcast.105, bf16[2048,1024]{1,0:T(8,128)(2,1)} %get-tuple-element.26.tok_ref, f32[3072]{0:T(1024)S(1)} %copy-done.31, f32[3072]{0:T(1024)S(1)} %pad_maximum_fusion), kind=kOutput, calls=%fused_computation.1 | convolution fusion | flops 12903776256 | bytes 23093248 | tf_op jit(solution)/shard_map/dot_general | solution.py:347
  145.8 32.2 %attend.1 = (bf16[1024,2048]{1,0:T(8,128)(2,1)S(1)}, f32[2,8,2048]{2,1,0:T(8,128)S(1)}) custom-call(s32[8]{0:T(128)S(1)} %get-tuple-element.62.lo_ref, s32[8]{0:T(128)S(1)} %get-tuple-element.63.hi_ref, bf16[3072,2048]{1,0:T(8,128)(2,1)} %multiply_convert_fusion.q_ref.k_ref.v_ref, bf16[3072,2048]{1,0:T(8,128)(2,1)} %multiply_convert_fusion.q_ref.k_ref.v_ref, ...), custom_call_target="tpu_custom_call" | custom-call | flops 20000000000 | bytes 14000000 | tf_op jit(solution)/shard_map/attend/pallas_call | solution.py:513
  178.1 2.8 fusion.8
  181.0 1.1 multiply_reduce_fusion.3
  182.0 2.7 fusion.7.x_ref.norm_ref
  184.7 19.5 %feed_up.1 = (bf16[1024,4096]{1,0:T(8,128)(2,1)}, bf16[1024,4096]{1,0:T(8,128)(2,1)}) custom-call(bf16[1024,1024]{1,0:T(8,128)(2,1)} %fusion.7.x_ref.norm_ref, bf16[4096,1024]{1,0:T(8,128)(2,1)} %bitcast.103, f32[1,4096]{1,0:T(1,128)} %reshape_reshape.6.bias_ref), custom_call_target="tpu_custom_call" | custom-call | flops 8589934592 | bytes 26000000 | tf_op jit(solution)/shard_map/feed_up/pallas_call | solution.py:641
  204.2 9.0 %stack_chunks.1 = bf16[4,2,4,8,16,1024]{5,4,3,2,1,0:T(8,128)(2,1)} custom-call(bf16[2,8,2,4,4,16,512]{6,5,4,3,2,1,0:T(8,128)(2,1)} %bitcast.67), custom_call_target="tpu_custom_call" | custom-call | bytes 17000000 | tf_op jit(solution)/shard_map/stack_chunks/pallas_call | solution.py:1061
  213.2 15.0 %fusion.33 = (f32[1024]{0:T(1024)S(1)}, f32[1024,1024]{1,0:T(8,128)S(1)}) fusion(f32[1024]{0:T(1024)S(1)} %bitcast.100, bf16[1024,4096]{1,0:T(8,128)(2,1)} %get-tuple-element.30.hid_ref, bf16[4096,1024]{1,0:T(8,128)(2,1)} %bitcast.68, f32[1024]{0:T(1024)S(1)} %bitcast.97, f32[1024]{0:T(1024)S(1)} %bitcast.83, f32[1024]{0:T(1024)S(1)} %add_rsqrt_fusion.1, ...), kind=kOutput, calls=%fused_computation.95 | convolution fusion | flops 8601467904 | bytes 25194496 | tf_op jit(solution)/shard_map/dot_general | solution.py:347
  228.2 0.5 multiply_reduce_fusion.2
  228.7 1.0 copy-done.15
  229.7 2.2 fusion.6
  232.0 3.0 fusion.30
  235.0 0.3 convert_element_type.76.g_ref.two_ref
  235.3 13.7 %feed_down_back.1 = (bf16[1024,4096]{1,0:T(8,128)(2,1)S(1)}, f32[1,4096]{1,0:T(1,128)S(1)}) custom-call(bf16[1024,1024]{1,0:T(8,128)(2,1)S(1)} %convert_element_type.76.g_ref.two_ref, bf16[4096,1024]{1,0:T(8,128)(2,1)} %bitcast.69, bf16[1024,4096]{1,0:T(8,128)(2,1)} %get-tuple-element.32.slope_ref), custom_call_target="tpu_custom_call" | custom-call | flops 8589934592 | bytes 26000000 | tf_op jit(solution)/shard_map/feed_down_back/pallas_call | solution.py:675
  249.1 14.2 %fusion.34 = f32[1024,1024]{1,0:T(8,128)S(1)} fusion(bf16[1024,4096]{1,0:T(8,128)(2,1)S(1)} %get-tuple-element.33.pre_ref, bf16[4096,1024]{1,0:T(8,128)(2,1)} %bitcast.104), kind=kOutput, calls=%fused_computation.96 | convolution fusion | flops 8589934592 | bytes 20971520 | tf_op jit(solution)/shard_map/dot_general | solution.py:347
  263.4 3.3 multiply_reduce_fusion
  266.7 0.5 broadcast_in_dim.120
  267.2 3.2 convert_dynamic-update-slice_fusion.1
  270.4 1.9 copy-done.16
  272.4 2.6 reduce_sum.193
  275.0 0.5 broadcast_in_dim.119
  275.5 1.7 copy-done.10
  277.2 2.4 convert_dynamic-update-slice_fusion.g_ref
  279.6 2.0 copy-done.17
  281.6 62.2 %attend_back.1 = (bf16[3,1024,2048]{2,1,0:T(8,128)(2,1)}, f32[2,1024,128]{2,1,0:T(8,128)}) custom-call(s32[8]{0:T(128)} %copy-done.4, s32[8]{0:T(128)} %copy-done.5, bf16[3072,2048]{1,0:T(8,128)(2,1)} %multiply_convert_fusion.q_ref.k_ref.v_ref, bf16[3072,2048]{1,0:T(8,128)(2,1)} %multiply_convert_fusion.q_ref.k_ref.v_ref, ...), custom_call_target="tpu_custom_call" | custom-call | flops 49999998976 | bytes 30000000 | tf_op jit(solution)/shard_map/attend_back/pallas_call | solution.py:550
  343.9 1.6 copy.29
  345.4 0.5 broadcast.178
  345.9 0.7 reduce.3
  346.7 1.3 concatenate.15.vec_ref
  348.0 190.2 %reduce_grads.1 = (bf16[6,128,1024]{2,1,0:T(8,128)(2,1)}, f32[12,1024]{1,0:T(8,128)}, bf16[2048,1024]{1,0:T(8,128)(2,1)}, bf16[800,1024]{1,0:T(8,128)(2,1)}) custom-call(s32[96]{0:T(128)} %scatter_custom_fusion.piece_ref, f32[12,1024]{1,0:T(8,128)} %concatenate.15.vec_ref, bf16[3,1024,2048]{2,1,0:T(8,128)(2,1)} %get-tuple-element.37.qkv_ref, ...), custom_call_target="tpu_custom_call" | custom-call | flops 41000001536 | bytes 50000000 | tf_op jit(solution)/shard_map/reduce_grads/pallas_call | solution.py:1518
  538.2 0.3 broadcast_in_dim.121
  538.4 1.8 constant_dynamic-update-slice_fusion
  540.2 0.6 copy-done.11
  540.8 4.3 add_convert_fusion
  545.2 0.9 copy-done.19
  546.1 6.1 %fusion.16 = (f32[1,6,128,1024]{3,2,1,0:T(8,128)}, f32[1,6,128,1024]{3,2,1,0:T(8,128)}, f32[1,6,128,1024]{3,2,1,0:T(8,128)}) fusion(bf16[6,128,1024]{2,1,0:T(8,128)(2,1)S(1)} %copy-done.20, f32[1,6,128,1024]{3,2,1,0:T(8,128)S(1)} %copy-done.18, f32[1,6,128,1024]{3,2,1,0:T(8,128)S(1)} %copy-done.19, f32[1,6,128,1024]{3,2,1,0:T(8,128)S(1)} %copy-done.14), kind=kLoop, calls=%fused_computation.36 | loop fusion | flops 11796480 | bytes 20447232 | tf_op jit(solution)/shard_map/broadcast_in_dim | solution.py:1720
  552.2 0.7 multiply_subtract_fusion
  (90 shorter events, 0.4 us)
Async XLA Ops:
  7.2 118.2 %copy-start.31 = (f32[3072]{0:T(1024)S(1)}, f32[3072]{0:T(1024)}, u32[]{:S(2)}) copy-start(f32[3072]{0:T(1024)} %constant.86.clone.1) | copy-start | bytes 36868
  7.2 116.4 %copy-start.28 = (s32[48,1]{0,1:T(1,128)S(1)}, s32[48,1]{0,1:T(1,128)}, u32[]{:S(2)}) copy-start(s32[48,1]{0,1:T(1,128)} %param.14) | copy-start | bytes 580
  7.2 115.2 %copy-start.23 = (s32[1,2048]{1,0:T(1,128)S(1)}, s32[1,2048]{1,0:T(1,128)}, u32[]{:S(2)}) copy-start(s32[1,2048]{1,0:T(1,128)} %param.12) | copy-start | bytes 24580
  7.2 115.7 %copy-start.21 = (f32[12,1024]{1,0:T(8,128)S(1)}, f32[12,1024]{1,0:T(8,128)}, u32[]{:S(2)}) copy-start(f32[12,1024]{1,0:T(8,128)} %param.18) | copy-start | bytes 147460
  7.2 118.0 %copy-start.27 = (s32[1,2048]{1,0:T(1,128)S(1)}, s32[1,2048]{1,0:T(1,128)}, u32[]{:S(2)}) copy-start(s32[1,2048]{1,0:T(1,128)} %param.13) | copy-start | bytes 24580
  7.2 196.9 %all-gather.3.cloned.1.call-start = ((), (), s32[]{:S(2)}) async-start(), calls=%async_computation | async-start | bytes 8650752 | tf_op jit(solution)/shard_map/all_gather | solution.py:1621
  125.2 20.6 %copy-start.4 = (s32[8]{0:T(128)}, s32[8]{0:T(128)S(1)}, u32[]{:S(2)}) copy-start(s32[8]{0:T(128)S(1)} %get-tuple-element.62.lo_ref) | copy-start | bytes 100
  125.2 20.6 %copy-start.5 = (s32[8]{0:T(128)}, s32[8]{0:T(128)S(1)}, u32[]{:S(2)}) copy-start(s32[8]{0:T(128)S(1)} %get-tuple-element.63.hi_ref) | copy-start | bytes 100
  125.4 20.4 %copy-start.1 = (bf16[16,2048]{1,0:T(8,128)(2,1)}, bf16[16,2048]{1,0:T(8,128)(2,1)S(1)}, u32[]{:S(2)}) copy-start(bf16[16,2048]{1,0:T(8,128)(2,1)S(1)} %get-tuple-element.76.kaug_ref) | copy-start | bytes 196612
  125.4 20.4 %copy-start.2 = (bf16[16,2048]{1,0:T(8,128)(2,1)}, bf16[16,2048]{1,0:T(8,128)(2,1)S(1)}, u32[]{:S(2)}) copy-start(bf16[16,2048]{1,0:T(8,128)(2,1)S(1)} %get-tuple-element.77.qaug_ref) | copy-start | bytes 196612
  145.8 32.3 %copy-start.3 = (f32[8,2048]{1,0:T(8,128)}, f32[8,2048]{1,0:T(8,128)S(1)}, u32[]{:S(2)}) copy-start(f32[8,2048]{1,0:T(8,128)S(1)} %broadcast_in_dim.117.hid_ref) | copy-start | bytes 196612
  145.8 32.3 %copy-start.9 = (bf16[1024,1024]{1,0:T(8,128)(2,1)S(1)}, bf16[1024,1024]{1,0:T(8,128)(2,1)}, u32[]{:S(2)}) copy-start(bf16[1024,1024]{1,0:T(8,128)(2,1)} %tokens_ref.1) | copy-start | bytes 6291460
  145.8 32.3 %copy-start.29 = (bf16[1,2,4,128,1024]{4,3,2,1,0:T(8,128)(2,1)S(1)}, bf16[1,2,4,128,1024]{4,3,2,1,0:T(8,128)(2,1)}, u32[]{:S(2)}) copy-start(bf16[1,2,4,128,1024]{4,3,2,1,0:T(8,128)(2,1)} %get-tuple-element.28) | copy-start | bytes 6291460
  178.1 2.8 copy-start.7
  178.1 2.8 copy-start.8
  180.9 3.8 copy-start.12
  228.1 1.6 copy-start.15
  235.3 13.7 %copy-start = (bf16[1024,1024]{1,0:T(8,128)(2,1)}, bf16[1024,1024]{1,0:T(8,128)(2,1)S(1)}, u32[]{:S(2)}) copy-start(bf16[1024,1024]{1,0:T(8,128)(2,1)S(1)} %convert_element_type.76.g_ref.two_ref) | copy-start | bytes 6291460
  249.1 14.3 %copy-start.6 = (bf16[1024,4096]{1,0:T(8,128)(2,1)}, bf16[1024,4096]{1,0:T(8,128)(2,1)S(1)}, u32[]{:S(2)}) copy-start(bf16[1024,4096]{1,0:T(8,128)(2,1)S(1)} %get-tuple-element.33.pre_ref) | copy-start | bytes 25165828
  249.1 14.3 %copy-start.13 = (bf16[1024,1024]{1,0:T(8,128)(2,1)S(1)}, bf16[1024,1024]{1,0:T(8,128)(2,1)}, u32[]{:S(2)}) copy-start(bf16[1024,1024]{1,0:T(8,128)(2,1)} %copy-done.12) | copy-start | bytes 6291460
  270.4 1.9 copy-start.16
  272.4 3.1 copy-start.30
  275.0 2.2 copy-start.10
  279.6 2.0 copy-start.17
  538.2 2.7 copy-start.11
  538.4 6.7 %copy-start.20 = (bf16[6,128,1024]{2,1,0:T(8,128)(2,1)S(1)}, bf16[6,128,1024]{2,1,0:T(8,128)(2,1)}, u32[]{:S(2)}) copy-start(bf16[6,128,1024]{2,1,0:T(8,128)(2,1)} %get-tuple-element.40) | copy-start | bytes 4718596
  540.8 4.3 copy-start.14
  540.8 4.3 copy-start.18
  540.8 5.2 copy-start.19
  546.1 6.1 %copy-start.22 = (f32[12,1024]{1,0:T(8,128)S(1)}, f32[12,1024]{1,0:T(8,128)}, u32[]{:S(2)}) copy-start(f32[12,1024]{1,0:T(8,128)} %param.18) | copy-start | bytes 147460
  546.1 6.1 %copy-start.24 = (f32[12,1024]{1,0:T(8,128)S(1)}, f32[12,1024]{1,0:T(8,128)}, u32[]{:S(2)}) copy-start(f32[12,1024]{1,0:T(8,128)} %param.19) | copy-start | bytes 147460
  546.1 6.1 %copy-start.25 = (f32[12,1024]{1,0:T(8,128)S(1)}, f32[12,1024]{1,0:T(8,128)}, u32[]{:S(2)}) copy-start(f32[12,1024]{1,0:T(8,128)} %param.20) | copy-start | bytes 147460
  546.1 6.1 %copy-start.26 = (f32[12,1024]{1,0:T(8,128)S(1)}, f32[12,1024]{1,0:T(8,128)}, u32[]{:S(2)}) copy-start(f32[12,1024]{1,0:T(8,128)} %get-tuple-element.41) | copy-start | bytes 147460
Sparse Core Ops, SparseCore 0:
  122.5 78.1 all-gather.2

commit v3 on v2

--- a/solution.py
+++ b/solution.py
@@ -1075,7 +1075,7 @@
 BLOCKS = 12
 SLICES = 2
 STEPS = BLOCKS * SLICES
-LAG = 2
+LAG = 3
 
 
 def reduce_kernel(

time: 568 us -> 566 us (level)
    pallas_call x1, Pallas kernels: 190 us -> 175 us  [reduce_grads(): pl.pallas_call(reduce_kernel, out_shape=(jax.ShapeDtypeStruct((CAP, 128,...]
    pallas_call x1, Pallas kernels: 62.2 us -> 73.8 us  [attend_back(): pl.pallas_call(attn_bwd_kernel, out_shape=(jax.ShapeDtypeStruct((3, D, ex...]
    pallas_call x1, Pallas kernels: 32.2 us -> 39 us  [attend(): pl.pallas_call(attn_fwd_kernel, out_shape=(jax.ShapeDtypeStruct((D, ext),...]
  transfers between devices with their start and end apart: 1 -> 1, of which waited for: 0 -> 0; matrix products, arithmetic and copies ran while one was open for 5% -> 5% of each run, Pallas kernels for 9% -> 10%
where the time goes in v3:
time: 566 us; the launch traced here: 563 us
  Pallas kernels  445 us (79%)
  matrix products  54.7 us (10%)
  other arithmetic  31.5 us (6%)
  local copies, waits for them, and re-layouts  16.9 us (3%)
  between operations  14.9 us (3%)
    pallas_call x1, Pallas kernels, reduce_grads(): pl.pallas_call(reduce_kernel, out_shape=(jax.ShapeDtypeStruct((CAP, 128,...  175 us
    pallas_call x1, Pallas kernels, gather_weights(): pl.pallas_call(gather_kernel, out_shape=tuple((jax.ShapeDtypeStruct((coun...  115 us
    pallas_call x1, Pallas kernels, attend_back(): pl.pallas_call(attn_bwd_kernel, out_shape=(jax.ShapeDtypeStruct((3, D, ex...  73.8 us
    dot_general x5, matrix products, mm(): return lax.dot_general(a, b, dims, preferred_element_type=jnp.float32)  54.7 us
    pallas_call x1, Pallas kernels, attend(): pl.pallas_call(attn_fwd_kernel, out_shape=(jax.ShapeDtypeStruct((D, ext),...  39 us
    pallas_call x1, Pallas kernels, feed_up(): pl.pallas_call(up_kernel, out_shape=(out, out), grid=(units // UNITS,), i...  19.6 us
    pallas_call x1, Pallas kernels, feed_down_back(): pl.pallas_call(down_back_kernel, out_shape=(jax.ShapeDtypeStruct((length,...  13.7 us
  transfers between devices with their start and end apart: 1, of which 0 were waited for; matrix products, arithmetic and copies ran while one was open for 5% of the time, Pallas kernels for 10%

profile of v3, /device:TPU:13, one launch (start us, length us, event | category | flops | bytes accessed | tf_op | source)
XLA Modules:
  0.0 563.5 jit_solution(7590148056026380809)
XLA Ops:
  7.2 0.0 all-gather.3.cloned.1.call-start
  7.3 115.1 %gather_weights.1 = (bf16[3,2,4,128,1024]{4,3,2,1,0:T(8,128)(2,1)}, bf16[1,2,4,128,1024]{4,3,2,1,0:T(8,128)(2,1)}, bf16[4,2,4,128,1024]{4,3,2,1,0:T(8,128)(2,1)}...) custom-call(s32[48]{0:T(128)} %bitcast.101, f32[6,128,1024]{2,1,0:T(8,128)} %bitcast.66, bf16[1024,1024]{1,0:T(8,128)(2,1)} %tokens_ref.1), custom_call_target="tpu_custom_call" | custom-call | bytes 50000000 | tf_op jit(solution)/shard_map/gather_weights/pallas_call | solution.py:1013
  122.4 0.2 convert_reduce_fusion.1
  122.6 0.1 select_reduce_fusion
  122.7 0.1 pad.5.clone
  122.8 0.1 pad.4.clone
  122.9 0.6 reshape_reshape.6.bias_ref
  123.6 0.2 convert_reduce_fusion.3
  123.7 1.2 scatter_custom_fusion.piece_ref
  125.0 0.2 select_reduce_fusion.2
  125.3 0.1 maximum_maximum_fusion.1
  125.4 20.4 %multiply_convert_fusion.q_ref.k_ref.v_ref = bf16[3072,2048]{1,0:T(8,128)(2,1)} fusion(bf16[3072,1024]{1,0:T(8,128)(2,1)} %bitcast.105, bf16[2048,1024]{1,0:T(8,128)(2,1)} %get-tuple-element.26.tok_ref, f32[3072]{0:T(1024)S(1)} %copy-done.31, f32[3072]{0:T(1024)S(1)} %pad_maximum_fusion), kind=kOutput, calls=%fused_computation.1 | convolution fusion | flops 12903776256 | bytes 23093248 | tf_op jit(solution)/shard_map/dot_general | solution.py:347
  145.8 39.0 %attend.1 = (bf16[1024,2048]{1,0:T(8,128)(2,1)S(1)}, f32[2,8,2048]{2,1,0:T(8,128)S(1)}) custom-call(s32[8]{0:T(128)S(1)} %get-tuple-element.62.lo_ref, s32[8]{0:T(128)S(1)} %get-tuple-element.63.hi_ref, bf16[3072,2048]{1,0:T(8,128)(2,1)} %multiply_convert_fusion.q_ref.k_ref.v_ref, bf16[3072,2048]{1,0:T(8,128)(2,1)} %multiply_convert_fusion.q_ref.k_ref.v_ref, ...), custom_call_target="tpu_custom_call" | custom-call | flops 20000000000 | bytes 14000000 | tf_op jit(solution)/shard_map/attend/pallas_call | solution.py:513
  184.9 2.8 fusion.8
  187.8 1.1 multiply_reduce_fusion.3
  188.8 2.7 fusion.7.x_ref.norm_ref
  191.5 19.6 %feed_up.1 = (bf16[1024,4096]{1,0:T(8,128)(2,1)}, bf16[1024,4096]{1,0:T(8,128)(2,1)}) custom-call(bf16[1024,1024]{1,0:T(8,128)(2,1)} %fusion.7.x_ref.norm_ref, bf16[4096,1024]{1,0:T(8,128)(2,1)} %bitcast.103, f32[1,4096]{1,0:T(1,128)} %reshape_reshape.6.bias_ref), custom_call_target="tpu_custom_call" | custom-call | flops 8589934592 | bytes 26000000 | tf_op jit(solution)/shard_map/feed_up/pallas_call | solution.py:641
  211.1 9.0 %stack_chunks.1 = bf16[4,2,4,8,16,1024]{5,4,3,2,1,0:T(8,128)(2,1)} custom-call(bf16[2,8,2,4,4,16,512]{6,5,4,3,2,1,0:T(8,128)(2,1)} %bitcast.67), custom_call_target="tpu_custom_call" | custom-call | bytes 17000000 | tf_op jit(solution)/shard_map/stack_chunks/pallas_call | solution.py:1061
  220.1 15.0 %fusion.33 = (f32[1024]{0:T(1024)S(1)}, f32[1024,1024]{1,0:T(8,128)S(1)}) fusion(f32[1024]{0:T(1024)S(1)} %bitcast.100, bf16[1024,4096]{1,0:T(8,128)(2,1)} %get-tuple-element.30.hid_ref, bf16[4096,1024]{1,0:T(8,128)(2,1)} %bitcast.68, f32[1024]{0:T(1024)S(1)} %bitcast.97, f32[1024]{0:T(1024)S(1)} %bitcast.83, f32[1024]{0:T(1024)S(1)} %add_rsqrt_fusion.1, ...), kind=kOutput, calls=%fused_computation.95 | convolution fusion | flops 8601467904 | bytes 25194496 | tf_op jit(solution)/shard_map/dot_general | solution.py:347
  235.1 0.5 multiply_reduce_fusion.2
  235.7 1.0 copy-done.15
  236.7 2.2 fusion.6
  239.0 3.0 fusion.30
  242.0 0.3 convert_element_type.76.g_ref.two_ref
  242.3 13.7 %feed_down_back.1 = (bf16[1024,4096]{1,0:T(8,128)(2,1)S(1)}, f32[1,4096]{1,0:T(1,128)S(1)}) custom-call(bf16[1024,1024]{1,0:T(8,128)(2,1)S(1)} %convert_element_type.76.g_ref.two_ref, bf16[4096,1024]{1,0:T(8,128)(2,1)} %bitcast.69, bf16[1024,4096]{1,0:T(8,128)(2,1)} %get-tuple-element.32.slope_ref), custom_call_target="tpu_custom_call" | custom-call | flops 8589934592 | bytes 26000000 | tf_op jit(solution)/shard_map/feed_down_back/pallas_call | solution.py:675
  256.1 14.2 %fusion.34 = f32[1024,1024]{1,0:T(8,128)S(1)} fusion(bf16[1024,4096]{1,0:T(8,128)(2,1)S(1)} %get-tuple-element.33.pre_ref, bf16[4096,1024]{1,0:T(8,128)(2,1)} %bitcast.104), kind=kOutput, calls=%fused_computation.96 | convolution fusion | flops 8589934592 | bytes 20971520 | tf_op jit(solution)/shard_map/dot_general | solution.py:347
  270.3 3.3 multiply_reduce_fusion
  273.6 0.5 broadcast_in_dim.120
  274.2 3.2 convert_dynamic-update-slice_fusion.1
  277.4 1.9 copy-done.16
  279.3 2.6 reduce_sum.193
  282.0 0.5 broadcast_in_dim.119
  282.5 1.7 copy-done.10
  284.2 2.4 convert_dynamic-update-slice_fusion.g_ref
  286.6 2.0 copy-done.17
  288.6 73.8 %attend_back.1 = (bf16[3,1024,2048]{2,1,0:T(8,128)(2,1)}, f32[2,1024,128]{2,1,0:T(8,128)}) custom-call(s32[8]{0:T(128)} %copy-done.4, s32[8]{0:T(128)} %copy-done.5, bf16[3072,2048]{1,0:T(8,128)(2,1)} %multiply_convert_fusion.q_ref.k_ref.v_ref, bf16[3072,2048]{1,0:T(8,128)(2,1)} %multiply_convert_fusion.q_ref.k_ref.v_ref, ...), custom_call_target="tpu_custom_call" | custom-call | flops 49999998976 | bytes 30000000 | tf_op jit(solution)/shard_map/attend_back/pallas_call | solution.py:550
  362.4 1.6 copy.29
  364.0 0.5 broadcast.178
  364.5 0.7 reduce.3
  365.3 1.3 concatenate.15.vec_ref
  366.6 175.2 %reduce_grads.1 = (bf16[6,128,1024]{2,1,0:T(8,128)(2,1)}, f32[12,1024]{1,0:T(8,128)}, bf16[2048,1024]{1,0:T(8,128)(2,1)}, bf16[800,1024]{1,0:T(8,128)(2,1)}) custom-call(s32[96]{0:T(128)} %scatter_custom_fusion.piece_ref, f32[12,1024]{1,0:T(8,128)} %concatenate.15.vec_ref, bf16[3,1024,2048]{2,1,0:T(8,128)(2,1)} %get-tuple-element.37.qkv_ref, ...), custom_call_target="tpu_custom_call" | custom-call | flops 41000001536 | bytes 50000000 | tf_op jit(solution)/shard_map/reduce_grads/pallas_call | solution.py:1518
  541.8 0.3 broadcast_in_dim.121
  542.0 1.8 constant_dynamic-update-slice_fusion
  543.8 0.6 copy-done.11
  544.4 4.3 add_convert_fusion
  548.8 0.9 copy-done.19
  549.7 6.1 %fusion.16 = (f32[1,6,128,1024]{3,2,1,0:T(8,128)}, f32[1,6,128,1024]{3,2,1,0:T(8,128)}, f32[1,6,128,1024]{3,2,1,0:T(8,128)}) fusion(bf16[6,128,1024]{2,1,0:T(8,128)(2,1)S(1)} %copy-done.20, f32[1,6,128,1024]{3,2,1,0:T(8,128)S(1)} %copy-done.18, f32[1,6,128,1024]{3,2,1,0:T(8,128)S(1)} %copy-done.19, f32[1,6,128,1024]{3,2,1,0:T(8,128)S(1)} %copy-done.14), kind=kLoop, calls=%fused_computation.36 | loop fusion | flops 11796480 | bytes 20447232 | tf_op jit(solution)/shard_map/broadcast_in_dim | solution.py:1720
  555.8 0.7 multiply_subtract_fusion
  (90 shorter events, 0.4 us)
Async XLA Ops:
  7.2 118.2 %copy-start.31 = (f32[3072]{0:T(1024)S(1)}, f32[3072]{0:T(1024)}, u32[]{:S(2)}) copy-start(f32[3072]{0:T(1024)} %constant.86.clone.1) | copy-start | bytes 36868
  7.2 116.4 %copy-start.28 = (s32[48,1]{0,1:T(1,128)S(1)}, s32[48,1]{0,1:T(1,128)}, u32[]{:S(2)}) copy-start(s32[48,1]{0,1:T(1,128)} %param.14) | copy-start | bytes 580
  7.2 115.2 %copy-start.23 = (s32[1,2048]{1,0:T(1,128)S(1)}, s32[1,2048]{1,0:T(1,128)}, u32[]{:S(2)}) copy-start(s32[1,2048]{1,0:T(1,128)} %param.12) | copy-start | bytes 24580
  7.2 115.7 %copy-start.21 = (f32[12,1024]{1,0:T(8,128)S(1)}, f32[12,1024]{1,0:T(8,128)}, u32[]{:S(2)}) copy-start(f32[12,1024]{1,0:T(8,128)} %param.18) | copy-start | bytes 147460
  7.2 118.0 %copy-start.27 = (s32[1,2048]{1,0:T(1,128)S(1)}, s32[1,2048]{1,0:T(1,128)}, u32[]{:S(2)}) copy-start(s32[1,2048]{1,0:T(1,128)} %param.13) | copy-start | bytes 24580
  7.2 203.9 %all-gather.3.cloned.1.call-start = ((), (), s32[]{:S(2)}) async-start(), calls=%async_computation | async-start | bytes 8650752 | tf_op jit(solution)/shard_map/all_gather | solution.py:1621
  125.2 20.6 %copy-start.4 = (s32[8]{0:T(128)}, s32[8]{0:T(128)S(1)}, u32[]{:S(2)}) copy-start(s32[8]{0:T(128)S(1)} %get-tuple-element.62.lo_ref) | copy-start | bytes 100
  125.2 20.6 %copy-start.5 = (s32[8]{0:T(128)}, s32[8]{0:T(128)S(1)}, u32[]{:S(2)}) copy-start(s32[8]{0:T(128)S(1)} %get-tuple-element.63.hi_ref) | copy-start | bytes 100
  125.4 20.4 %copy-start.1 = (bf16[16,2048]{1,0:T(8,128)(2,1)}, bf16[16,2048]{1,0:T(8,128)(2,1)S(1)}, u32[]{:S(2)}) copy-start(bf16[16,2048]{1,0:T(8,128)(2,1)S(1)} %get-tuple-element.76.kaug_ref) | copy-start | bytes 196612
  125.4 20.4 %copy-start.2 = (bf16[16,2048]{1,0:T(8,128)(2,1)}, bf16[16,2048]{1,0:T(8,128)(2,1)S(1)}, u32[]{:S(2)}) copy-start(bf16[16,2048]{1,0:T(8,128)(2,1)S(1)} %get-tuple-element.77.qaug_ref) | copy-start | bytes 196612
  145.8 39.1 %copy-start.3 = (f32[8,2048]{1,0:T(8,128)}, f32[8,2048]{1,0:T(8,128)S(1)}, u32[]{:S(2)}) copy-start(f32[8,2048]{1,0:T(8,128)S(1)} %broadcast_in_dim.117.hid_ref) | copy-start | bytes 196612
  145.8 39.1 %copy-start.9 = (bf16[1024,1024]{1,0:T(8,128)(2,1)S(1)}, bf16[1024,1024]{1,0:T(8,128)(2,1)}, u32[]{:S(2)}) copy-start(bf16[1024,1024]{1,0:T(8,128)(2,1)} %tokens_ref.1) | copy-start | bytes 6291460
  145.8 39.1 %copy-start.29 = (bf16[1,2,4,128,1024]{4,3,2,1,0:T(8,128)(2,1)S(1)}, bf16[1,2,4,128,1024]{4,3,2,1,0:T(8,128)(2,1)}, u32[]{:S(2)}) copy-start(bf16[1,2,4,128,1024]{4,3,2,1,0:T(8,128)(2,1)} %get-tuple-element.28) | copy-start | bytes 6291460
  184.9 2.8 copy-start.7
  184.9 2.8 copy-start.8
  187.8 3.8 copy-start.12
  235.1 1.6 copy-start.15
  242.3 13.7 %copy-start = (bf16[1024,1024]{1,0:T(8,128)(2,1)}, bf16[1024,1024]{1,0:T(8,128)(2,1)S(1)}, u32[]{:S(2)}) copy-start(bf16[1024,1024]{1,0:T(8,128)(2,1)S(1)} %convert_element_type.76.g_ref.two_ref) | copy-start | bytes 6291460
  256.0 14.3 %copy-start.6 = (bf16[1024,4096]{1,0:T(8,128)(2,1)}, bf16[1024,4096]{1,0:T(8,128)(2,1)S(1)}, u32[]{:S(2)}) copy-start(bf16[1024,4096]{1,0:T(8,128)(2,1)S(1)} %get-tuple-element.33.pre_ref) | copy-start | bytes 25165828
  256.1 14.3 %copy-start.13 = (bf16[1024,1024]{1,0:T(8,128)(2,1)S(1)}, bf16[1024,1024]{1,0:T(8,128)(2,1)}, u32[]{:S(2)}) copy-start(bf16[1024,1024]{1,0:T(8,128)(2,1)} %copy-done.12) | copy-start | bytes 6291460
  277.4 1.9 copy-start.16
  279.3 3.1 copy-start.30
  282.0 2.2 copy-start.10
  286.6 2.0 copy-start.17
  541.8 2.7 copy-start.11
  542.0 6.7 %copy-start.20 = (bf16[6,128,1024]{2,1,0:T(8,128)(2,1)S(1)}, bf16[6,128,1024]{2,1,0:T(8,128)(2,1)}, u32[]{:S(2)}) copy-start(bf16[6,128,1024]{2,1,0:T(8,128)(2,1)} %get-tuple-element.40) | copy-start | bytes 4718596
  544.4 4.3 copy-start.14
  544.4 4.3 copy-start.18
  544.4 5.2 copy-start.19
  549.7 6.1 %copy-start.22 = (f32[12,1024]{1,0:T(8,128)S(1)}, f32[12,1024]{1,0:T(8,128)}, u32[]{:S(2)}) copy-start(f32[12,1024]{1,0:T(8,128)} %param.18) | copy-start | bytes 147460
  549.7 6.1 %copy-start.24 = (f32[12,1024]{1,0:T(8,128)S(1)}, f32[12,1024]{1,0:T(8,128)}, u32[]{:S(2)}) copy-start(f32[12,1024]{1,0:T(8,128)} %param.19) | copy-start | bytes 147460
  549.7 6.1 %copy-start.25 = (f32[12,1024]{1,0:T(8,128)S(1)}, f32[12,1024]{1,0:T(8,128)}, u32[]{:S(2)}) copy-start(f32[12,1024]{1,0:T(8,128)} %param.20) | copy-start | bytes 147460
  549.7 6.1 %copy-start.26 = (f32[12,1024]{1,0:T(8,128)S(1)}, f32[12,1024]{1,0:T(8,128)}, u32[]{:S(2)}) copy-start(f32[12,1024]{1,0:T(8,128)} %get-tuple-element.41) | copy-start | bytes 147460
Sparse Core Ops, SparseCore 0:
  122.5 78.0 all-gather.2
